TPU v7x, 32 devices: a whole 2x2x4 slice. The times are simulated.
32 devices in a mesh: row: 4 (over z), col: 8 (over y, x, core).
Axes of the slice: x: 2, y: 2, z: 4, core: 2. Of those that a mesh axis runs over, the one named last changes fastest.
Arguments:
- dens_real: float32 [8192, 8192], P('row', 'col'), as said below
- dens_imag: float32 [8192, 8192], P('row', 'col'), as said below
- upper_band: float32 [8192, 384], P('row'), may hold values from -0.3 to 0.3
- pattern: int32 [64, 2], P('row'), may hold values 0 or 1
Outputs:
- new_real: float32 [8192, 8192], P('row', 'col')
- new_imag: float32 [8192, 8192], P('row', 'col')
Inputs may be any that keep to these rules, and one draw needn't show every extreme that they name: dens_real is symmetric. dens_imag is antisymmetric, with a zero diagonal.
All inputs are finite; a program needn't handle non-finite values. No bound on the sum of `pattern` on one device may be relied on, other than what follows from the above.
Results may differ from a plain program's by a relative error of at most 0.0001.
Values sent between devices are 32-bit elements; how exact they have to be, the bound alone decides.
No kernel may reach another device: no remote copies, remote signals or barrier semaphores. Data moves between devices by JAX's collectives and lax.ppermute only.
A program may use at most 192 MiB of HBM per device.

v0:
```python
import jax
import jax.numpy as jnp
from jax import lax
from jax.sharding import PartitionSpec as P

BS = 128
KB = 2
NB = 64


HIGHEST_PRECISION = lax.Precision.HIGHEST
STEP_TIME = 0.3


def extended(x, sides, width):
    for axis, dim in sides:
        devices, length = (lax.axis_size(axis), x.shape[dim])
        up = [(i, (i + 1) % devices) for i in range(devices - 1)]
        down = [(j, i) for i, j in up]
        last = lax.slice_in_dim(x, length - width, length, axis=dim)
        leading = lax.slice_in_dim(x, 0, width, axis=dim)
        before = lax.ppermute(last, axis, up)
        after = lax.ppermute(leading, axis, down)
        x = jnp.concatenate([before, x, after], axis=dim)
    return x


def from_behind(x, axis, by):
    devices = lax.axis_size(axis)
    pairs = [(i, i + by) for i in range(devices) if 0 <= i + by < devices]
    return lax.ppermute(x, axis, pairs)


def spread(value, axis, source):
    kept = jnp.where(lax.axis_index(axis) == source, value, 0).astype(value.dtype)
    return lax.psum(kept, axis)


def masked_band(upper_band, pattern, first_block):
    block_count = pattern.shape[0]
    blocks = upper_band.reshape(block_count, BS, KB + 1, BS)
    block_index = first_block + jnp.arange(block_count, dtype=jnp.int32)
    offsets = jnp.arange(1, KB + 1, dtype=jnp.int32)
    present = (pattern > 0) & (block_index[:, None] + offsets[None, :] < NB)
    factor = jnp.concatenate(
        [jnp.ones((block_count, 1), jnp.float32), present.astype(jnp.float32)], axis=1
    )
    return (blocks * factor[:, None, :, None]).reshape(block_count * BS, (KB + 1) * BS)


def build_tiles(masked_ext, block_count):
    blocks = masked_ext.reshape(block_count + KB, BS, KB + 1, BS)
    tile_list = []
    for k in range(2 * KB + 1):
        offset_block = k - KB
        if offset_block < 0:
            distance = -offset_block
            piece_rows = blocks[KB - distance : KB - distance + block_count, :, distance, :]
            tile_list.append(jnp.swapaxes(piece_rows, 1, 2))
        elif offset_block == 0:
            piece_rows = blocks[KB:, :, 0, :]
            tile_list.append(0.5 * (piece_rows + jnp.swapaxes(piece_rows, 1, 2)))
        else:
            tile_list.append(blocks[KB:, :, offset_block, :])
    return jnp.stack(tile_list, axis=2)


def group_matrix(tile_set):
    group_blocks = 2 * KB
    group_count = tile_set.shape[0] // group_blocks
    window_blocks = group_blocks + 2 * KB
    grouped = tile_set.reshape(group_count, group_blocks, BS, (2 * KB + 1) * BS)
    strips = []
    for lead in range(group_blocks):
        tail = window_blocks - (2 * KB + 1) - lead
        strips.append(jnp.pad(grouped[:, lead], ((0, 0), (0, 0), (lead * BS, tail * BS))))
    return jnp.stack(strips, axis=1).reshape(group_count, group_blocks * BS, window_blocks * BS)


def row_product(dense_groups, rows_ext):
    group_count = dense_groups.shape[0]
    group_rows = dense_groups.shape[1]
    window_rows = dense_groups.shape[2]
    windows = jnp.stack(
        [rows_ext[g * group_rows : g * group_rows + window_rows] for g in range(group_count)],
        axis=0,
    )
    summed = jnp.einsum("grw,gwn->grn", dense_groups, windows, precision=HIGHEST_PRECISION)
    return summed.reshape(group_count * group_rows, rows_ext.shape[1])


def column_product(dense_groups, columns_ext):
    group_count = dense_groups.shape[0]
    group_rows = dense_groups.shape[1]
    window_rows = dense_groups.shape[2]
    windows = jnp.stack(
        [columns_ext[:, g * group_rows : g * group_rows + window_rows] for g in range(group_count)],
        axis=0,
    )
    summed = jnp.einsum("gnw,grw->ngr", windows, dense_groups, precision=HIGHEST_PRECISION)
    return summed.reshape(columns_ext.shape[0], group_count * group_rows)


def commutators(real_rows, real_columns, imag_rows, imag_columns, row_tiles, column_tiles):
    row_dense = group_matrix(row_tiles)
    column_dense = group_matrix(column_tiles)
    h_real = row_product(row_dense, real_rows)
    h_imag = row_product(row_dense, imag_rows)
    real_h = column_product(column_dense, real_columns)
    imag_h = column_product(column_dense, imag_columns)
    return (h_imag - imag_h, real_h - h_real)


def section_slope(real_part, imag_part, row_tiles, column_tiles):
    rim_width = KB * BS
    padded_real, padded_imag = (
        extended(real_part, (("row", 0), ("col", 1)), rim_width),
        extended(imag_part, (("row", 0), ("col", 1)), rim_width),
    )
    return commutators(
        padded_real[:, rim_width:-rim_width],
        padded_real[rim_width:-rim_width, :],
        padded_imag[:, rim_width:-rim_width],
        padded_imag[rim_width:-rim_width, :],
        row_tiles,
        column_tiles,
    )


def shards(dens_real, dens_imag, upper_band, pattern):
    rim_width = KB * BS
    row_blocks = dens_real.shape[0] // BS
    column_blocks = dens_real.shape[1] // BS
    panel_first = lax.axis_index("row") * row_blocks
    masked = masked_band(upper_band, pattern, panel_first)
    per_row = lax.axis_size("col") // lax.axis_size("row")
    source_row = lax.axis_index("col") // per_row
    column_first = lax.axis_index("col") * column_blocks
    offset_rows = (column_first - source_row * row_blocks) * BS
    above_rows = from_behind(masked[-rim_width:], "row", 1)
    panel_rows = jnp.concatenate([above_rows, masked], axis=0)
    row_tiles = build_tiles(panel_rows, row_blocks)
    column_panel = spread(panel_rows, "row", source_row)
    column_band = lax.dynamic_slice_in_dim(column_panel, offset_rows, (column_blocks + KB) * BS, 0)
    column_tiles = build_tiles(column_band, column_blocks)
    slope_real, slope_imag = section_slope(dens_real, dens_imag, row_tiles, column_tiles)
    section_real = dens_real + STEP_TIME * slope_real
    section_imag = dens_imag + STEP_TIME * slope_imag
    second_real, second_imag = section_slope(section_real, section_imag, row_tiles, column_tiles)
    new_real = dens_real + 0.5 * STEP_TIME * (slope_real + second_real)
    new_imag = dens_imag + 0.5 * STEP_TIME * (slope_imag + second_imag)
    return (new_real, new_imag)


def solution(mesh):
    in_specs = (P("row", "col"), P("row", "col"), P("row", None), P("row", None))
    out_specs = (P("row", "col"), P("row", "col"))
    return jax.shard_map(shards, mesh=mesh, in_specs=in_specs, out_specs=out_specs, check_vma=False)
```

profile of v0, /device:TPU:1, one launch (start us, length us, event | category | flops | bytes accessed | tf_op | source)
XLA Modules:
  0.0 702.0 jit_solution(1236093099432177045)
XLA Ops:
  11.6 5.6 collective-permute-start.5
  35.3 33.9 %collective-permute-done = f32[256,384]{0,1:T(8,128)} collective-permute-done((f32[256,384]{0,1:T(8,128)S(1)}, f32[256,384]{0,1:T(8,128)}, u32[]{:S(2)}, u32[]{:S(2)}) %collective-permute-start) | collective-permute-done | bytes 393248 | tf_op jit(solution)/shard_map/ppermute | solution.py:31
  99.0 8.8 %copy.36 = f32[4,4,128,1024]{3,2,1,0:T(8,128)} copy(f32[4,4,128,1024]{2,3,0,1:T(8,128)} %pad_maximum_fusion.16) | data formatting | bytes 16777216 | tf_op jit(solution)/shard_map/stack | solution.py:77
  125.0 8.0 %fusion.69 = (f32[1,1024,1024]{2,1,0:T(8,128)}, f32[1,1024,1024]{2,1,0:T(8,128)}, f32[1,1024,1024]{2,1,0:T(8,128)}, f32[1,1024,1024]{2,1,0:T(8,128)}) fusion(f32[2048,1024]{1,0:T(8,128)S(1)} %bitcast.221, f32[256,1024]{1,0:T(8,128)} %collective-permute-done.1, f32[256,1024]{1,0:T(8,128)} %collective-permute-done.2), kind=kLoop, calls=%fused_computation.105 | loop fusion | flops 2097152 | bytes 35651584 | tf_op jit(solution)/shard_map/stack | solution.py:84
  133.0 13.1 %fusion.67 = (f32[1,1024,1024]{2,1,0:T(8,128)}, f32[1,1024,1024]{2,1,0:T(8,128)}, f32[1,1024,1024]{2,1,0:T(8,128)}, f32[1,1024,1024]{2,1,0:T(8,128)}) fusion(f32[2048,1024]{1,0:T(8,128)} %param.4, f32[256,1024]{1,0:T(8,128)} %collective-permute-done.5, f32[256,1024]{1,0:T(8,128)} %collective-permute-done.6), kind=kLoop, calls=%fused_computation.101 | loop fusion | flops 2097152 | bytes 35651584 | tf_op jit(solution)/shard_map/stack | solution.py:84
  148.5 32.9 %fusion = f32[4,512,1024]{2,1,0:T(8,128)} fusion(f32[4,512,1024]{2,1,0:T(8,128)S(1)} %bitcast.208, f32[1,1024,1024]{2,1,0:T(8,128)} %get-tuple-element.31, f32[1,1024,1024]{2,1,0:T(8,128)} %get-tuple-element.29, f32[1,1024,1024]{2,1,0:T(8,128)} %get-tuple-element.30, f32[1,1024,1024]{2,1,0:T(8,128)S(1)} %copy-done.5), kind=kOutput, calls=%fused_computation | convolution fusion | flops 25782386688 | bytes 33554432 | tf_op jit(solution)/shard_map/grw,gwn->grn/dot_general | solution.py:88
  181.4 33.6 %fusion.16 = f32[4,512,1024]{2,1,0:T(8,128)} fusion(f32[4,512,1024]{2,1,0:T(8,128)S(1)} %bitcast.209, f32[1,1024,1024]{2,1,0:T(8,128)} %get-tuple-element.43, f32[1,1024,1024]{2,1,0:T(8,128)} %get-tuple-element.41, f32[1,1024,1024]{2,1,0:T(8,128)} %get-tuple-element.42, f32[1,1024,1024]{2,1,0:T(8,128)} %get-tuple-element.40), kind=kOutput, calls=%fused_computation.16 | convolution fusion | flops 25782386688 | bytes 33554432 | tf_op jit(solution)/shard_map/grw,gwn->grn/dot_general | solution.py:88
  215.0 11.5 %fusion.55 = (f32[1,2048,1024]{2,1,0:T(8,128)}, f32[1,2048,1024]{2,1,0:T(8,128)}) fusion(f32[2560,1024]{1,0:T(8,128)} %copy-done.4, f32[2560,256]{1,0:T(8,128)} %collective-permute-done.3, f32[2560,256]{1,0:T(8,128)} %collective-permute-done.4), kind=kLoop, calls=%fused_computation.71 | loop fusion | flops 4194304 | bytes 32505856 | tf_op jit(solution)/shard_map/stack | solution.py:96
  251.8 5.4 copy.46
  257.1 32.6 %fusion.8 = f32[2,512,2048]{2,1,0:T(8,128)} fusion(f32[2,512,1024]{2,1,0:T(8,128)} %bitcast.216, f32[1,2048,1024]{2,1,0:T(8,128)} %get-tuple-element.9, f32[1,2048,1024]{2,1,0:T(8,128)} %get-tuple-element.8), kind=kOutput, calls=%fused_computation.8 | convolution fusion | flops 25773998080 | bytes 29360128 | tf_op jit(solution)/shard_map/gnw,grw->ngr/dot_general | solution.py:100
  289.8 9.2 %copy.47 = f32[2048,1024]{1,0:T(8,128)} copy(f32[2048,1024]{0,1:T(8,128)} %bitcast.223) | data formatting | bytes 16777216 | tf_op jit(solution)/shard_map/reshape | solution.py:101
  299.0 13.6 %multiply_add_fusion = (f32[2048,1024]{1,0:T(8,128)S(1)}, f32[2560,1024]{1,0:T(8,128)}) fusion(f32[2048,1024]{1,0:T(8,128)} %param.4, f32[2048,1024]{1,0:T(8,128)} %copy.47, f32[4,512,1024]{2,1,0:T(8,128)} %fusion, f32[2560,1024]{1,0:T(8,128)} %constant_dynamic-update-slice_fusion.5), kind=kLoop, calls=%fused_computation.83 | loop fusion | flops 6291456 | bytes 41943040 | tf_op jit(solution)/shard_map/add | solution.py:147
  321.1 5.2 fusion.82
  332.1 8.0 %collective-permute-done.13 = f32[256,1024]{1,0:T(8,128)S(1)} collective-permute-done((f32[256,1024]{1,0:T(8,128)S(1)}, f32[256,1024]{1,0:T(8,128)S(1)}, u32[]{:S(2)}, u32[]{:S(2)}) %collective-permute-start.13) | collective-permute-done | bytes 1048608 | tf_op jit(solution)/shard_map/ppermute | solution.py:22
  353.4 11.0 %fusion.63 = (f32[1,1024,1024]{2,1,0:T(8,128)S(1)}, f32[1,1024,1024]{2,1,0:T(8,128)}, f32[1,1024,1024]{2,1,0:T(8,128)}, f32[1,1024,1024]{2,1,0:T(8,128)}) fusion(f32[2048,1024]{1,0:T(8,128)} %copy-done.3, f32[256,1024]{1,0:T(8,128)S(1)} %collective-permute-done.13, f32[256,1024]{1,0:T(8,128)S(1)} %collective-permute-done.14), kind=kLoop, calls=%fused_computation.91 | loop fusion | flops 2097152 | bytes 35651584 | tf_op jit(solution)/shard_map/stack | solution.py:84
  364.4 33.0 %fusion.40 = f32[4,512,1024]{2,1,0:T(8,128)} fusion(f32[4,512,1024]{2,1,0:T(8,128)S(1)} %bitcast.212, f32[1,1024,1024]{2,1,0:T(8,128)} %get-tuple-element.23, f32[1,1024,1024]{2,1,0:T(8,128)} %get-tuple-element.21, f32[1,1024,1024]{2,1,0:T(8,128)} %get-tuple-element.22, f32[1,1024,1024]{2,1,0:T(8,128)S(1)} %get-tuple-element.20), kind=kOutput, calls=%fused_computation.40 | convolution fusion | flops 25782386688 | bytes 33554432 | tf_op jit(solution)/shard_map/grw,gwn->grn/dot_general | solution.py:88
  397.4 9.7 %fusion.53 = (f32[1,2048,1024]{2,1,0:T(8,128)S(1)}, f32[1,2048,1024]{2,1,0:T(8,128)}) fusion(f32[2560,1024]{1,0:T(8,128)} %constant_dynamic-update-slice_fusion.3, f32[2560,256]{1,0:T(8,128)} %collective-permute-done.7, f32[2560,256]{1,0:T(8,128)} %collective-permute-done.8), kind=kLoop, calls=%fused_computation.67 | loop fusion | flops 4194304 | bytes 32505856 | tf_op jit(solution)/shard_map/stack | solution.py:96
  407.1 31.0 %fusion.12 = f32[2,512,2048]{2,1,0:T(8,128)} fusion(f32[2,512,1024]{2,1,0:T(8,128)S(1)} %bitcast.217, f32[1,2048,1024]{2,1,0:T(8,128)} %get-tuple-element.17, f32[1,2048,1024]{2,1,0:T(8,128)S(1)} %get-tuple-element.16), kind=kOutput, calls=%fused_computation.12 | convolution fusion | flops 25773998080 | bytes 29360128 | tf_op jit(solution)/shard_map/gnw,grw->ngr/dot_general | solution.py:100
  438.1 9.3 %copy.48 = f32[2048,1024]{1,0:T(8,128)} copy(f32[2048,1024]{0,1:T(8,128)} %bitcast.224) | data formatting | bytes 16777216 | tf_op jit(solution)/shard_map/reshape | solution.py:101
  447.5 11.6 %fusion.49 = (f32[1,2048,1024]{2,1,0:T(8,128)}, f32[1,2048,1024]{2,1,0:T(8,128)}) fusion(f32[2560,256]{1,0:T(8,128)} %collective-permute-done.15, f32[256,1024]{1,0:T(8,128)S(1)} %copy-done.7, f32[2048,1024]{1,0:T(8,128)} %copy-done.3, f32[256,1024]{1,0:T(8,128)S(1)} %collective-permute-done.13, f32[2560,256]{1,0:T(8,128)} %collective-permute-done.16), kind=kLoop, calls=%fused_computation.53 | loop fusion | flops 12582912 | bytes 32505856 | tf_op jit(solution)/shard_map/stack | solution.py:96
  459.1 31.6 %fusion.36 = f32[2,512,2048]{2,1,0:T(8,128)} fusion(f32[2,512,1024]{2,1,0:T(8,128)S(1)} %bitcast.218, f32[1,2048,1024]{2,1,0:T(8,128)} %get-tuple-element.5, f32[1,2048,1024]{2,1,0:T(8,128)} %get-tuple-element.4), kind=kOutput, calls=%fused_computation.36 | convolution fusion | flops 25773998080 | bytes 29360128 | tf_op jit(solution)/shard_map/gnw,grw->ngr/dot_general | solution.py:100
  490.6 9.2 %copy.52 = f32[2048,1024]{1,0:T(8,128)} copy(f32[2048,1024]{0,1:T(8,128)} %bitcast.225) | data formatting | bytes 16777216 | tf_op jit(solution)/shard_map/reshape | solution.py:101
  499.9 22.9 %fusion.58 = (f32[2048,1024]{1,0:T(8,128)}, f32[2048,1024]{1,0:T(8,128)}) fusion(f32[2048,1024]{1,0:T(8,128)} %param.5, f32[2048,1024]{1,0:T(8,128)} %copy.52, f32[4,512,1024]{2,1,0:T(8,128)} %fusion.40, f32[2048,1024]{1,0:T(8,128)} %copy.48, f32[4,512,1024]{2,1,0:T(8,128)} %fusion.16), kind=kLoop, calls=%fused_computation.76 | loop fusion | flops 14680064 | bytes 58720256 | tf_op jit(solution)/shard_map/add | solution.py:151
  529.2 21.3 %collective-permute-done.9 = f32[256,1024]{1,0:T(8,128)S(1)} collective-permute-done((f32[256,1024]{1,0:T(8,128)S(1)}, f32[256,1024]{1,0:T(8,128)S(1)}, u32[]{:S(2)}, u32[]{:S(2)}) %collective-permute-start.9) | collective-permute-done | bytes 1048608 | tf_op jit(solution)/shard_map/ppermute | solution.py:22
  554.5 5.5 pad_maximum_fusion.34
  566.2 10.9 %fusion.65 = (f32[1,1024,1024]{2,1,0:T(8,128)S(1)}, f32[1,1024,1024]{2,1,0:T(8,128)}, f32[1,1024,1024]{2,1,0:T(8,128)}, f32[1,1024,1024]{2,1,0:T(8,128)}) fusion(f32[2048,1024]{1,0:T(8,128)} %get-tuple-element.3, f32[256,1024]{1,0:T(8,128)S(1)} %collective-permute-done.9, f32[256,1024]{1,0:T(8,128)S(1)} %collective-permute-done.10), kind=kLoop, calls=%fused_computation.97 | loop fusion | flops 2097152 | bytes 35651584 | tf_op jit(solution)/shard_map/stack | solution.py:84
  577.2 33.0 %fusion.24 = f32[4,512,1024]{2,1,0:T(8,128)} fusion(f32[4,512,1024]{2,1,0:T(8,128)S(1)} %bitcast.215, f32[1,1024,1024]{2,1,0:T(8,128)} %get-tuple-element.35, f32[1,1024,1024]{2,1,0:T(8,128)} %get-tuple-element.36, f32[1,1024,1024]{2,1,0:T(8,128)} %get-tuple-element.37, f32[1,1024,1024]{2,1,0:T(8,128)S(1)} %get-tuple-element.34), kind=kOutput, calls=%fused_computation.24 | convolution fusion | flops 25782386688 | bytes 33554432 | tf_op jit(solution)/shard_map/grw,gwn->grn/dot_general | solution.py:88
  610.2 12.9 %collective-permute-done.12 = f32[2560,256]{1,0:T(8,128)} collective-permute-done((f32[2560,256]{1,0:T(8,128)}, f32[2560,256]{1,0:T(8,128)}, u32[]{:S(2)}, u32[]{:S(2)}) %collective-permute-start.12) | collective-permute-done | bytes 2621472 | tf_op jit(solution)/shard_map/ppermute | solution.py:23
  623.1 11.2 %fusion.51 = (f32[1,2048,1024]{2,1,0:T(8,128)}, f32[1,2048,1024]{2,1,0:T(8,128)}) fusion(f32[2560,256]{1,0:T(8,128)} %collective-permute-done.11, f32[256,1024]{1,0:T(8,128)} %copy-done.8, f32[2048,1024]{1,0:T(8,128)} %get-tuple-element.3, f32[256,1024]{1,0:T(8,128)S(1)} %collective-permute-done.9, f32[2560,256]{1,0:T(8,128)} %collective-permute-done.12), kind=kLoop, calls=%fused_computation.61 | loop fusion | flops 12582912 | bytes 32505856 | tf_op jit(solution)/shard_map/stack | solution.py:96
  634.3 31.7 %fusion.32 = f32[2,512,2048]{2,1,0:T(8,128)} fusion(f32[2,512,1024]{2,1,0:T(8,128)S(1)} %bitcast.219, f32[1,2048,1024]{2,1,0:T(8,128)} %get-tuple-element.13, f32[1,2048,1024]{2,1,0:T(8,128)} %get-tuple-element.12), kind=kOutput, calls=%fused_computation.32 | convolution fusion | flops 25773998080 | bytes 29360128 | tf_op jit(solution)/shard_map/gnw,grw->ngr/dot_general | solution.py:100
  666.0 9.2 %copy.51 = f32[2048,1024]{1,0:T(8,128)} copy(f32[2048,1024]{0,1:T(8,128)} %bitcast.222) | data formatting | bytes 16777216 | tf_op jit(solution)/shard_map/reshape | solution.py:101
  675.3 19.6 %fusion.61 = f32[2048,1024]{1,0:T(8,128)} fusion(f32[2048,1024]{1,0:T(8,128)} %param.4, f32[2048,1024]{1,0:T(8,128)} %copy.51, f32[4,512,1024]{2,1,0:T(8,128)} %fusion.24, f32[2048,1024]{1,0:T(8,128)} %copy.47, f32[4,512,1024]{2,1,0:T(8,128)} %fusion), kind=kLoop, calls=%fused_computation.80 | loop fusion | flops 10485760 | bytes 50331648 | tf_op jit(solution)/shard_map/add | solution.py:150
  (123 shorter events, 140.9 us)
Async XLA Ops:
  7.2 19.6 %copy-start.9 = (s32[16,2]{0,1:T(2,128)S(1)}, s32[16,2]{0,1:T(2,128)}, u32[]{:S(2)}) copy-start(s32[16,2]{0,1:T(2,128)} %param.7) | copy-start | bytes 388
  7.2 219.3 %all-reduce.11.cloned.1.call-start = ((), (), s32[]{:S(2)}) async-start(), calls=%async_computation | async-start | bytes 7077888 | tf_op jit(solution)/shard_map/psum | solution.py:36
  10.3 122.6 %collective-permute-start.6 = (f32[256,1024]{1,0:T(8,128)}, f32[256,1024]{1,0:T(8,128)}, u32[]{:S(2)}, u32[]{:S(2)}) collective-permute-start(f32[256,1024]{1,0:T(8,128)} %get-tuple-element.44), channel_id=1, source_target_pairs={{8,0},{16,8},{24,16},{9,1},{17,9},{25,17},{10,2},{18,10},{26,18},{... | collective-permute-start | bytes 3145736 | tf_op jit(solution)/shard_map/ppermute | solution.py:23
  11.6 121.3 %collective-permute-start.5 = (f32[256,1024]{1,0:T(8,128)}, f32[256,1024]{1,0:T(8,128)}, u32[]{:S(2)}, u32[]{:S(2)}) collective-permute-start(f32[256,1024]{1,0:T(8,128)} %get-tuple-element.45), channel_id=1, source_target_pairs={{0,8},{8,16},{16,24},{1,9},{9,17},{17,25},{2,10},{10,18},{18,26},{... | collective-permute-start | bytes 3145736 | tf_op jit(solution)/shard_map/ppermute | solution.py:22
  20.4 93.3 %collective-permute-start.2 = (f32[256,1024]{1,0:T(8,128)}, f32[256,1024]{1,0:T(8,128)}, u32[]{:S(2)}, u32[]{:S(2)}) collective-permute-start(f32[256,1024]{1,0:T(8,128)} %get-tuple-element.32), channel_id=1, source_target_pairs={{8,0},{16,8},{24,16},{9,1},{17,9},{25,17},{10,2},{18,10},{26,18},{... | collective-permute-start | bytes 3145736 | tf_op jit(solution)/shard_map/ppermute | solution.py:23
  21.7 86.1 %collective-permute-start.1 = (f32[256,1024]{1,0:T(8,128)}, f32[256,1024]{1,0:T(8,128)}, u32[]{:S(2)}, u32[]{:S(2)}) collective-permute-start(f32[256,1024]{1,0:T(8,128)} %get-tuple-element.33), channel_id=1, source_target_pairs={{0,8},{8,16},{16,24},{1,9},{9,17},{17,25},{2,10},{10,18},{18,26},{... | collective-permute-start | bytes 3145736 | tf_op jit(solution)/shard_map/ppermute | solution.py:22
  30.2 39.0 %collective-permute-start = (f32[256,384]{0,1:T(8,128)S(1)}, f32[256,384]{0,1:T(8,128)}, u32[]{:S(2)}, u32[]{:S(2)}) collective-permute-start(f32[256,384]{0,1:T(8,128)S(1)} %bitcast.238), channel_id=1, source_target_pairs={{0,8},{8,16},{16,24},{1,9},{9,17},{17,25},{2,10},{10,18},{18,26},{... | collective-permute-start | bytes 1179656 | tf_op jit(solution)/shard_map/ppermute | solution.py:31
  107.8 17.2 %slice-start.6 = ((s8[8388608]{0:T(1024)(128)(4,1)}), s8[4194304]{0:T(1024)(128)(4,1)S(1)}, s32[]{:S(2)}) async-start(s8[8388608]{0:T(1024)(128)(4,1)} %bitcast.220), calls=%async_computation.7 | async-start | bytes 8388608
  109.2 15.8 %slice-start.7 = ((s8[8388608]{0:T(1024)(128)(4,1)}), s8[4194304]{0:T(1024)(128)(4,1)S(1)}, s32[]{:S(2)}) async-start(s8[8388608]{0:T(1024)(128)(4,1)} %bitcast.220), calls=%async_computation.8 | async-start | bytes 8388608
  118.0 96.9 %collective-permute-start.3 = (f32[2560,256]{1,0:T(8,128)}, f32[2560,256]{1,0:T(8,128)}, u32[]{:S(2)}, u32[]{:S(2)}) collective-permute-start(f32[2560,256]{1,0:T(8,128)} %get-tuple-element.10), channel_id=1, source_target_pairs={{0,1},{1,2},{2,3},{3,4},{4,5},{5,6},{6,7},{8,9},{9,10},{10,11},{11... | collective-permute-start | bytes 7864328 | tf_op jit(solution)/shard_map/ppermute | solution.py:22
  122.7 92.3 %collective-permute-start.4 = (f32[2560,256]{1,0:T(8,128)}, f32[2560,256]{1,0:T(8,128)}, u32[]{:S(2)}, u32[]{:S(2)}) collective-permute-start(f32[2560,256]{1,0:T(8,128)} %get-tuple-element.11), channel_id=1, source_target_pairs={{1,0},{2,1},{3,2},{4,3},{5,4},{6,5},{7,6},{9,8},{10,9},{11,10},{12... | collective-permute-start | bytes 7864328 | tf_op jit(solution)/shard_map/ppermute | solution.py:23
  125.0 23.5 %slice-start = ((s8[8388608]{0:T(1024)(128)(4,1)}), s8[4194304]{0:T(1024)(128)(4,1)S(1)}, s32[]{:S(2)}) async-start(s8[8388608]{0:T(1024)(128)(4,1)} %bitcast.206), calls=%async_computation.1 | async-start | bytes 8388608
  133.0 15.5 %slice-start.1 = ((s8[8388608]{0:T(1024)(128)(4,1)}), s8[4194304]{0:T(1024)(128)(4,1)S(1)}, s32[]{:S(2)}) async-start(s8[8388608]{0:T(1024)(128)(4,1)} %bitcast.206), calls=%async_computation.2 | async-start | bytes 8388608
  133.0 15.5 %copy-start.5 = (f32[1,1024,1024]{2,1,0:T(8,128)S(1)}, f32[1,1024,1024]{2,1,0:T(8,128)}, u32[]{:S(2)}) copy-start(f32[1,1024,1024]{2,1,0:T(8,128)} %get-tuple-element.28) | copy-start | bytes 12582916
  312.6 31.8 %copy-start.3 = (f32[2048,1024]{1,0:T(8,128)}, f32[2048,1024]{1,0:T(8,128)S(1)}, u32[]{:S(2)}) copy-start(f32[2048,1024]{1,0:T(8,128)S(1)} %get-tuple-element.26) | copy-start | bytes 25165828
  312.9 27.2 %collective-permute-start.13 = (f32[256,1024]{1,0:T(8,128)S(1)}, f32[256,1024]{1,0:T(8,128)S(1)}, u32[]{:S(2)}, u32[]{:S(2)}) collective-permute-start(f32[256,1024]{1,0:T(8,128)S(1)} %get-tuple-element.24), channel_id=1, source_target_pairs={{0,8},{8,16},{16,24},{1,9},{9,17},{17,25},{2,10},{10,18},{18,26},{... | collective-permute-start | bytes 3145736 | tf_op jit(solution)/shard_map/ppermute | solution.py:22
  317.4 27.0 %collective-permute-start.14 = (f32[256,1024]{1,0:T(8,128)S(1)}, f32[256,1024]{1,0:T(8,128)S(1)}, u32[]{:S(2)}, u32[]{:S(2)}) collective-permute-start(f32[256,1024]{1,0:T(8,128)S(1)} %get-tuple-element.25), channel_id=1, source_target_pairs={{8,0},{16,8},{24,16},{9,1},{17,9},{25,17},{10,2},{18,10},{26,18},{... | collective-permute-start | bytes 3145736 | tf_op jit(solution)/shard_map/ppermute | solution.py:23
  326.3 71.1 %collective-permute-start.7 = (f32[2560,256]{1,0:T(8,128)}, f32[2560,256]{1,0:T(8,128)}, u32[]{:S(2)}, u32[]{:S(2)}) collective-permute-start(f32[2560,256]{1,0:T(8,128)} %get-tuple-element.18), channel_id=1, source_target_pairs={{0,1},{1,2},{2,3},{3,4},{4,5},{5,6},{6,7},{8,9},{9,10},{10,11},{11... | collective-permute-start | bytes 7864328 | tf_op jit(solution)/shard_map/ppermute | solution.py:22
  330.1 67.3 %collective-permute-start.8 = (f32[2560,256]{1,0:T(8,128)}, f32[2560,256]{1,0:T(8,128)}, u32[]{:S(2)}, u32[]{:S(2)}) collective-permute-start(f32[2560,256]{1,0:T(8,128)} %get-tuple-element.19), channel_id=1, source_target_pairs={{1,0},{2,1},{3,2},{4,3},{5,4},{6,5},{7,6},{9,8},{10,9},{11,10},{12... | collective-permute-start | bytes 7864328 | tf_op jit(solution)/shard_map/ppermute | solution.py:23
  344.5 20.0 %copy-start.6 = (f32[256,1024]{1,0:T(8,128)}, f32[256,1024]{1,0:T(8,128)S(1)}, u32[]{:S(2)}) copy-start(f32[256,1024]{1,0:T(8,128)S(1)} %collective-permute-done.14) | copy-start | bytes 3145732
  347.3 100.2 %collective-permute-start.15 = (f32[2560,256]{1,0:T(8,128)}, f32[2560,256]{1,0:T(8,128)}, u32[]{:S(2)}, u32[]{:S(2)}) collective-permute-start(f32[2560,256]{1,0:T(8,128)} %get-tuple-element.6), channel_id=1, source_target_pairs={{0,1},{1,2},{2,3},{3,4},{4,5},{5,6},{6,7},{8,9},{9,10},{10,11},{11... | collective-permute-start | bytes 7864328 | tf_op jit(solution)/shard_map/ppermute | solution.py:22
  350.6 13.8 %slice-start.2 = ((s8[8388608]{0:T(1024)(128)(4,1)}), s8[4194304]{0:T(1024)(128)(4,1)S(1)}, s32[]{:S(2)}) async-start(s8[8388608]{0:T(1024)(128)(4,1)} %bitcast.210), calls=%async_computation.3 | async-start | bytes 8388608
  350.7 13.8 %slice-start.3 = ((s8[8388608]{0:T(1024)(128)(4,1)}), s8[4194304]{0:T(1024)(128)(4,1)S(1)}, s32[]{:S(2)}) async-start(s8[8388608]{0:T(1024)(128)(4,1)} %bitcast.210), calls=%async_computation.4 | async-start | bytes 8388608
  350.7 96.8 %collective-permute-start.16 = (f32[2560,256]{1,0:T(8,128)}, f32[2560,256]{1,0:T(8,128)}, u32[]{:S(2)}, u32[]{:S(2)}) collective-permute-start(f32[2560,256]{1,0:T(8,128)} %get-tuple-element.7), channel_id=1, source_target_pairs={{1,0},{2,1},{3,2},{4,3},{5,4},{6,5},{7,6},{9,8},{10,9},{11,10},{12... | collective-permute-start | bytes 7864328 | tf_op jit(solution)/shard_map/ppermute | solution.py:23
  524.5 26.0 %collective-permute-start.9 = (f32[256,1024]{1,0:T(8,128)S(1)}, f32[256,1024]{1,0:T(8,128)S(1)}, u32[]{:S(2)}, u32[]{:S(2)}) collective-permute-start(f32[256,1024]{1,0:T(8,128)S(1)} %get-tuple-element.38), channel_id=1, source_target_pairs={{0,8},{8,16},{16,24},{1,9},{9,17},{17,25},{2,10},{10,18},{18,26},{... | collective-permute-start | bytes 3145736 | tf_op jit(solution)/shard_map/ppermute | solution.py:22
  527.9 26.6 %collective-permute-start.10 = (f32[256,1024]{1,0:T(8,128)S(1)}, f32[256,1024]{1,0:T(8,128)S(1)}, u32[]{:S(2)}, u32[]{:S(2)}) collective-permute-start(f32[256,1024]{1,0:T(8,128)S(1)} %get-tuple-element.39), channel_id=1, source_target_pairs={{8,0},{16,8},{24,16},{9,1},{17,9},{25,17},{10,2},{18,10},{26,18},{... | collective-permute-start | bytes 3145736 | tf_op jit(solution)/shard_map/ppermute | solution.py:23
  554.5 22.7 %copy-start.8 = (f32[256,1024]{1,0:T(8,128)}, f32[256,1024]{1,0:T(8,128)S(1)}, u32[]{:S(2)}) copy-start(f32[256,1024]{1,0:T(8,128)S(1)} %collective-permute-done.10) | copy-start | bytes 3145732
  560.0 50.2 %collective-permute-start.11 = (f32[2560,256]{1,0:T(8,128)}, f32[2560,256]{1,0:T(8,128)}, u32[]{:S(2)}, u32[]{:S(2)}) collective-permute-start(f32[2560,256]{1,0:T(8,128)} %get-tuple-element.14), channel_id=1, source_target_pairs={{0,1},{1,2},{2,3},{3,4},{4,5},{5,6},{6,7},{8,9},{9,10},{10,11},{11... | collective-permute-start | bytes 7864328 | tf_op jit(solution)/shard_map/ppermute | solution.py:22
  563.6 13.6 %slice-start.4 = ((s8[8388608]{0:T(1024)(128)(4,1)}), s8[4194304]{0:T(1024)(128)(4,1)S(1)}, s32[]{:S(2)}) async-start(s8[8388608]{0:T(1024)(128)(4,1)} %bitcast.213), calls=%async_computation.5 | async-start | bytes 8388608
  563.6 13.6 %slice-start.5 = ((s8[8388608]{0:T(1024)(128)(4,1)}), s8[4194304]{0:T(1024)(128)(4,1)S(1)}, s32[]{:S(2)}) async-start(s8[8388608]{0:T(1024)(128)(4,1)} %bitcast.213), calls=%async_computation.6 | async-start | bytes 8388608
  563.6 59.5 %collective-permute-start.12 = (f32[2560,256]{1,0:T(8,128)}, f32[2560,256]{1,0:T(8,128)}, u32[]{:S(2)}, u32[]{:S(2)}) collective-permute-start(f32[2560,256]{1,0:T(8,128)} %get-tuple-element.15), channel_id=1, source_target_pairs={{1,0},{2,1},{3,2},{4,3},{5,4},{6,5},{7,6},{9,8},{10,9},{11,10},{12... | collective-permute-start | bytes 7864328 | tf_op jit(solution)/shard_map/ppermute | solution.py:23
  610.2 24.1 %copy-start.2 = (f32[2,4,128,1024]{3,2,1,0:T(8,128)S(1)}, f32[2,4,128,1024]{3,2,1,0:T(8,128)}, u32[]{:S(2)}) copy-start(f32[2,4,128,1024]{3,2,1,0:T(8,128)} %copy.46) | copy-start | bytes 12582916
  (4 other events, 38.4 us)
Sparse Core Ops, SparseCore 0:
  81.5 138.0 all-reduce.10
where the time goes:
time: 706 us; the launch traced here: 702 us
  matrix products  259 us (37%)
  other arithmetic  172 us (24%)
  local copies, waits for them, and re-layouts  120 us (17%)
  waiting for transfers between devices  84.5 us (12%)
  starting transfers between devices  52 us (7%)
  between operations  14.9 us (2%)
    dot_general x4, matrix products, row_product(): jnp.einsum('grw,gwn->grn', dense_groups, windows, precision=HIGHEST_PRECI...  132 us
    dot_general x4, matrix products, column_product(): jnp.einsum('gnw,grw->ngr', windows, dense_groups, precision=HIGHEST_PRECI...  127 us
    another operation x4, other arithmetic, column_product(): jnp.stack([columns_ext[:, g * group_rows:g * group_rows + window_rows] fo...  44 us
    another operation x4, other arithmetic, row_product(): jnp.stack([rows_ext[g * group_rows:g * group_rows + window_rows] for g in...  43 us
    reshape x4, local copies, waits for them, and re-layouts, column_product(): return summed.reshape(columns_ext.shape[0], group_count * group_rows)  37 us
    ppermute x8, starting transfers between devices, extended(): before = lax.ppermute(last, axis, up)  34.1 us
    ppermute x1, waiting for transfers between devices, from_behind(): return lax.ppermute(x, axis, pairs)  33.9 us
    ppermute x8, waiting for transfers between devices, extended(): before = lax.ppermute(last, axis, up)  29.3 us
  transfers between devices with their start and end apart: 18, of which 6 were waited for; matrix products, arithmetic and copies ran while one was open for 44% of the time, Pallas kernels for 0%

commit v1 on v0

v1 whole, which is shorter than its diff:
```python
import functools

import jax
import jax.numpy as jnp
from jax import lax
from jax.experimental import pallas as pl
from jax.experimental.pallas import tpu as pltpu
from jax.sharding import PartitionSpec as P

BS = 128
KB = 2
G = KB * BS
STEP_TIME = 0.3
F32 = jnp.float32
BF16 = jnp.bfloat16


def split(x):
    high = x.astype(BF16)
    low = (x - high.astype(F32)).astype(BF16)
    return high, low


def dot(a, b):
    return jnp.dot(a, b, preferred_element_type=F32)


def three(a_high, a_low, b_high, b_low):
    return dot(
        jnp.concatenate([a_high, a_low, a_high], axis=1),
        jnp.concatenate([b_high, b_high, b_low], axis=0),
    )


def band_kernel(transposed, u_ref, high_ref, low_ref):
    g = pl.program_id(0)
    first = pl.multiple_of(g * G, G)

    def upper(block, d):
        return u_ref[pl.ds(first + block * BS, BS), d * BS : (d + 1) * BS]

    for i in range(KB):
        for j in range(3 * KB):
            distance = (j - KB) - i
            if distance == 0:
                diag = upper(KB + i, 0)
                value = 0.5 * (diag + diag.T)
            elif 0 < distance <= KB:
                value = upper(KB + i, distance)
                value = value.T if transposed else value
            elif -KB <= distance < 0:
                value = upper(j, -distance)
                value = value if transposed else value.T
            else:
                value = jnp.zeros((BS, BS), F32)
            high, low = split(value)
            if transposed:
                at = (0, pl.ds(j * BS, BS), pl.ds(i * BS, BS))
            else:
                slot = lax.rem(g + 2 + j // KB, 3)
                column = pl.multiple_of(slot * G + (j % KB) * BS, BS)
                at = (0, pl.ds(i * BS, BS), pl.ds(column, BS))
            high_ref[at] = high
            low_ref[at] = low


def band_groups(u_ext, transposed):
    groups = u_ext.shape[0] // G - 1
    shape = (3 * G, G) if transposed else (G, 3 * G)
    out = jax.ShapeDtypeStruct((groups,) + shape, BF16)
    block = pl.BlockSpec((1,) + shape, lambda g: (g, 0, 0))
    return pl.pallas_call(
        functools.partial(band_kernel, transposed),
        grid=(groups,),
        in_specs=[pl.BlockSpec(u_ext.shape, lambda g: (0, 0))],
        out_specs=[block, block],
        out_shape=[out, out],
        compiler_params=pltpu.CompilerParams(vmem_limit_bytes=40 << 20),
        name="band_cols" if transposed else "band_rows",
    )(u_ext)


def load_ring(t, groups, p_ref, q_ref, ring):
    ph, pl_, qh, ql = ring
    slot = lax.rem(t, 3)

    @pl.when(t == 0)
    def _():
        for ref in ring:
            ref[2] = jnp.zeros(ref.shape[1:], BF16)

    @pl.when(t < groups)
    def _():
        ph[slot], pl_[slot] = split(p_ref[...])
        qh[slot], ql[slot] = split(q_ref[...])

    @pl.when(t == groups)
    def _():
        for ref in ring:
            ref[slot] = jnp.zeros(ref.shape[1:], BF16)


def left_product(both, xh, xl, at):
    w = dot(both, xh[:, :, at].reshape(3 * G, G))
    return w[:G] + w[G:] + dot(both[:G], xl[:, :, at].reshape(3 * G, G))


def right_product(lhs, n, columns, ch_ref, cl_ref):
    lo, hi = max(n - 1, 0) * G, min(n + 2, columns) * G
    k0 = lo - (n - 1) * G
    rows = lhs(slice(lo, hi))
    band = slice(k0, k0 + hi - lo)
    return three(rows[: 2 * G], rows[2 * G :], ch_ref[n, band, :], cl_ref[n, band, :])


def left_kernel(groups, p_ref, q_ref, hh_ref, hl_ref, po_ref, qo_ref, *ring):
    t = pl.program_id(0)
    load_ring(t, groups, p_ref, q_ref, ring)

    @pl.when(t > 0)
    def _():
        ph, pl_, qh, ql = ring
        both = jnp.concatenate([hh_ref[0], hl_ref[0]], axis=0)
        for n in range(ph.shape[2] // G):
            at = slice(n * G, (n + 1) * G)
            po_ref[:, at] = left_product(both, ph, pl_, at)
            qo_ref[:, at] = left_product(both, qh, ql, at)


def outer_kernel(side, p_ref, q_ref, h_ref, l_ref, halo_ref, pi_ref, qi_ref,
                 po_ref, qo_ref, rim_ref, rows):
    height = p_ref.shape[0]
    tile_at, halo_at = (slice(G, 3 * G), slice(0, 2 * G)), (slice(0, G), slice(2 * G, 3 * G))

    for k, x_ref in enumerate((p_ref, q_ref)):
        for half, value in enumerate(split(x_ref[...])):
            rows[k + 2 * half, :, tile_at[side]] = value
        for half, value in enumerate(split(halo_ref[k])):
            rows[k + 2 * half, :, halo_at[side]] = value
    high = rows[:2].reshape(2 * height, 3 * G)
    low = rows[2:].reshape(2 * height, 3 * G)
    right = three(high, low, h_ref[0], l_ref[0])
    p = pi_ref[...] - right[:height]
    q = qi_ref[...] - right[height:]
    po_ref[...] = p
    qo_ref[...] = q
    rim_ref[0], rim_ref[1] = p, q


def outer_columns(side, p, q, col_band, halo, p_left, q_left):
    height, width = p.shape
    rows = min(height, 2 * G)
    count, columns = height // rows, width // G
    band = pl.BlockSpec((1, 3 * G, G), lambda i: (side * (columns - 1), 0, 0))
    wide = pl.BlockSpec((rows, 2 * G), lambda i: (i, side * (columns // 2 - 1)))
    tile = pl.BlockSpec((rows, G), lambda i: (i, side * (columns - 1)))
    rim = pl.BlockSpec((2, rows, G), lambda i: (0, i, 0))
    out = jax.ShapeDtypeStruct(p.shape, F32)
    return pl.pallas_call(
        functools.partial(outer_kernel, side),
        grid=(count,),
        in_specs=[wide, wide, band, band, rim, tile, tile],
        out_specs=[tile, tile, rim],
        out_shape=[out, out, jax.ShapeDtypeStruct(halo.shape, F32)],
        input_output_aliases={5: 0, 6: 1},
        scratch_shapes=[pltpu.VMEM((4, rows, 3 * G), BF16)],
        compiler_params=pltpu.CompilerParams(vmem_limit_bytes=56 << 20),
        cost_estimate=pl.CostEstimate(flops=0, bytes_accessed=0, transcendentals=0),
        name="outer_columns",
    )(p, q, *col_band, halo, p_left, q_left)


def middle_kernel(groups, p_ref, q_ref, ch_ref, cl_ref, pi_ref, qi_ref,
                  po_ref, qo_ref, top_ref, bottom_ref, rows):
    i = pl.program_id(0)
    for k, x_ref in enumerate((p_ref, q_ref)):
        rows[k], rows[k + 2] = split(x_ref[...])
    columns = rows.shape[2] // G
    outs = ((pi_ref, po_ref), (qi_ref, qo_ref))
    for n in range(columns):
        at = slice(n * G, (n + 1) * G)
        if 0 < n < columns - 1:
            right = right_product(
                lambda w: rows[:, :, w].reshape(4 * G, w.stop - w.start), n, columns, ch_ref, cl_ref
            )
            for k, (i_ref, o_ref) in enumerate(outs):
                o_ref[:, at] = i_ref[:, at] - right[k * G : (k + 1) * G]
        else:
            for i_ref, o_ref in outs:
                o_ref[:, at] = i_ref[:, at]

    @pl.when(i == 0)
    def _():
        top_ref[0], top_ref[1] = po_ref[...], qo_ref[...]

    @pl.when(i == groups - 1)
    def _():
        bottom_ref[0], bottom_ref[1] = po_ref[...], qo_ref[...]


def middle_columns(p, q, col_band, p_left, q_left):
    height, width = p.shape
    groups = height // G
    tile = pl.BlockSpec((G, width), lambda i: (i, 0))
    band = pl.BlockSpec(col_band[0].shape, lambda i: (0, 0, 0))
    rim = pl.BlockSpec((2, G, width), lambda i: (0, 0, 0))
    out = jax.ShapeDtypeStruct(p.shape, F32)
    rim_out = jax.ShapeDtypeStruct((2, G, width), F32)
    return pl.pallas_call(
        functools.partial(middle_kernel, groups),
        grid=(groups,),
        in_specs=[tile, tile, band, band, tile, tile],
        out_specs=[tile, tile, rim, rim],
        out_shape=[out, out, rim_out, rim_out],
        input_output_aliases={4: 0, 5: 1},
        scratch_shapes=[pltpu.VMEM((4, G, width), BF16)],
        compiler_params=pltpu.CompilerParams(vmem_limit_bytes=56 << 20),
        cost_estimate=pl.CostEstimate(flops=0, bytes_accessed=0, transcendentals=0),
        name="middle_columns",
    )(p, q, *col_band, p_left, q_left)


def last_kernel(groups, p_ref, q_ref, hh_ref, hl_ref, ch_ref, cl_ref, pf_ref, qf_ref, a_ref, b_ref,
                po_ref, qo_ref, *ring):
    t = pl.program_id(0)
    load_ring(t, groups, p_ref, q_ref, ring)

    @pl.when(t > 0)
    def _():
        ph, pl_, qh, ql = ring
        mid = lax.rem(t + 2, 3)
        columns = ph.shape[2] // G
        both = jnp.concatenate([hh_ref[0], hl_ref[0]], axis=0)
        for n in range(columns):
            at = slice(n * G, (n + 1) * G)
            right = right_product(
                lambda w: jnp.concatenate([x[mid, :, w] for x in (ph, qh, pl_, ql)], axis=0),
                n, columns, ch_ref, cl_ref,
            )
            half_square = 0.5 * STEP_TIME * STEP_TIME
            slope = left_product(both, ph, pl_, at) - right[:G]
            po_ref[:, at] = a_ref[:, at] + STEP_TIME * qf_ref[:, at] - half_square * slope
            slope = left_product(both, qh, ql, at) - right[G:]
            qo_ref[:, at] = b_ref[:, at] - STEP_TIME * pf_ref[:, at] - half_square * slope


def ring_specs(p, groups):
    width = p.shape[1]
    ahead = pl.BlockSpec((G, width), lambda t: (jnp.minimum(t, groups - 1), 0))
    behind = pl.BlockSpec((G, width), lambda t: (jnp.maximum(t - 1, 0), 0))
    band = pl.BlockSpec((1, G, 3 * G), lambda t: (jnp.maximum(t - 1, 0), 0, 0))
    return ahead, behind, band, [pltpu.VMEM((3, G, width), BF16)] * 4


def from_left(p, q, row_band):
    groups = p.shape[0] // G
    ahead, behind, band, ring = ring_specs(p, groups)
    out = jax.ShapeDtypeStruct(p.shape, F32)
    return pl.pallas_call(
        functools.partial(left_kernel, groups),
        grid=(groups + 1,),
        in_specs=[ahead, ahead, band, band],
        out_specs=[behind, behind],
        out_shape=[out, out],
        scratch_shapes=ring,
        compiler_params=pltpu.CompilerParams(vmem_limit_bytes=56 << 20),
        cost_estimate=pl.CostEstimate(flops=0, bytes_accessed=0, transcendentals=0),
        name="from_left",
    )(p, q, *row_band)


def inner(p, q, row_band, col_band, a, b):
    groups = p.shape[0] // G
    ahead, behind, band, ring = ring_specs(p, groups)
    whole = pl.BlockSpec(col_band[0].shape, lambda t: (0, 0, 0))
    out = jax.ShapeDtypeStruct(p.shape, F32)
    return pl.pallas_call(
        functools.partial(last_kernel, groups),
        grid=(groups + 1,),
        in_specs=[ahead, ahead, band, band, whole, whole] + [behind] * 4,
        out_specs=[behind, behind],
        out_shape=[out, out],
        scratch_shapes=ring,
        compiler_params=pltpu.CompilerParams(vmem_limit_bytes=56 << 20),
        cost_estimate=pl.CostEstimate(flops=0, bytes_accessed=0, transcendentals=0),
        name="inner",
    )(p, q, *row_band, *col_band, p, q, a, b)


def row_edge_kernel(scale, h_ref, l_ref, above_ref, below_ref, p_ref, q_ref, *refs):
    outs, rims = (refs[1:3], refs[3:]) if len(refs) > 2 else (refs, ())
    high, low = h_ref[0], l_ref[0]
    both = jnp.concatenate([high, low], axis=0)

    def add(halo_ref):
        for k, (x_ref, o_ref) in enumerate(zip((p_ref, q_ref), outs)):
            xh, xl = split(halo_ref[k])
            w = dot(both, xh)
            value = x_ref[...] + scale * (w[:G] + w[G:] + dot(high, xl))
            o_ref[...] = value
            for rim in rims:
                rim[k] = value[:, :G]

    pl.when(pl.program_id(0) == 0)(lambda: add(above_ref))
    pl.when(pl.program_id(0) == 1)(lambda: add(below_ref))


def row_edges(p, q, above, below, edge_band, scale, rims=()):
    height, width = p.shape
    groups = height // G
    band = pl.BlockSpec((1, G, G), lambda s: (s, 0, 0))
    halo = pl.BlockSpec(above.shape, lambda s: (0, 0, 0))
    tile = pl.BlockSpec((G, width), lambda s: (s * (groups - 1), 0))
    rim = pl.BlockSpec((2, G, G), lambda s: (0, s * (groups - 1), 0))
    out = jax.ShapeDtypeStruct(p.shape, F32)
    return pl.pallas_call(
        functools.partial(row_edge_kernel, scale),
        grid=(2,),
        in_specs=[band, band, halo, halo, tile, tile] + [rim for _ in rims],
        out_specs=[tile, tile] + [rim for _ in rims],
        out_shape=[out, out] + [jax.ShapeDtypeStruct(x.shape, F32) for x in rims],
        input_output_aliases={4 + k: k for k in range(2 + len(rims))},
        compiler_params=pltpu.CompilerParams(vmem_limit_bytes=40 << 20),
        name="row_edges",
    )(*edge_band, above, below, p, q, *rims)


def col_edge_kernel(scale, relayed, with_rim, use_ref, *refs):
    h_ref, l_ref, before_ref, after_ref = refs[:4]
    refs = refs[4:]
    if relayed:
        extra_ref, refs = refs[0], refs[1:]
    p_ref, q_ref, po_ref, qo_ref = refs[:4]
    rim = refs[4:]
    s = pl.program_id(0)
    high, low = h_ref[0], l_ref[0]

    def add(halo_ref, side):
        rows = halo_ref.shape[1]
        halo = halo_ref[...].reshape(2 * rows, G)
        if relayed:
            halo = jnp.where(use_ref[side] > 0, extra_ref[...].reshape(2 * rows, G), halo)
        xh, xl = split(halo)
        w = dot(jnp.concatenate([xh, xl], axis=0), high)
        w = w[: 2 * rows] + w[2 * rows :] + dot(xh, low)
        for k, (x_ref, o_ref) in enumerate(((p_ref, po_ref), (q_ref, qo_ref))):
            value = x_ref[...] - scale * w[k * rows : (k + 1) * rows]
            o_ref[...] = value
            if with_rim:
                rim[side][k] = value

    pl.when(s == 0)(lambda: add(before_ref, 0))
    pl.when(s == 1)(lambda: add(after_ref, 1))


def col_edges(p, q, halos, edge_band, scale, use, groups, with_rim):
    before, after, extra = halos
    width = p.shape[1]
    first, step, count = groups
    columns = width // G
    rows = G
    if first == 0 and step == 1:
        rows = before.shape[1] // 4
        count = 4
    band = pl.BlockSpec((1, G, G), lambda s, i, use: (s, 0, 0))
    tile = pl.BlockSpec((rows, G), lambda s, i, use: (first + i * step, s * (columns - 1)))
    left = pl.BlockSpec((2, rows, G), lambda s, i, use: (0, jnp.where(s == 0, i, count - 1), 0))
    right = pl.BlockSpec((2, rows, G), lambda s, i, use: (0, jnp.where(s == 0, 0, i), 0))
    other = pl.BlockSpec((2, rows, G), lambda s, i, use: (0, i * use[s], 0))
    relayed = extra is not None
    out = jax.ShapeDtypeStruct(p.shape, F32)
    rim = jax.ShapeDtypeStruct(before.shape, F32)
    base = 5 + relayed
    return pl.pallas_call(
        functools.partial(col_edge_kernel, scale, relayed, with_rim),
        grid_spec=pltpu.PrefetchScalarGridSpec(
            num_scalar_prefetch=1,
            grid=(2, count),
            in_specs=[band, band, left, right] + [other] * relayed + [tile, tile],
            out_specs=[tile, tile] + ([left, right] if with_rim else []),
        ),
        out_shape=[out, out] + ([rim, rim] if with_rim else []),
        input_output_aliases={base: 0, base + 1: 1},
        compiler_params=pltpu.CompilerParams(vmem_limit_bytes=40 << 20),
        name="col_edges",
    )(use, *edge_band, before, after, *([extra] if relayed else []), p, q)


def chain(devices, by):
    return [(i, i + by) for i in range(devices) if 0 <= i + by < devices]


def swap_row_rims(top, bottom):
    devices = lax.axis_size("row")
    above = lax.ppermute(bottom, "row", chain(devices, 1))
    below = lax.ppermute(top, "row", chain(devices, -1))
    return above, below


def swap_col_rims(left, right, relayed):
    devices = lax.axis_size("col")
    half = devices // 2
    up, down = chain(devices, 1), chain(devices, -1)
    extra = None
    if relayed:
        up.remove((half - 1, half))
        down.remove((half, half - 1))
        mine = jnp.where(lax.axis_index("col") == half - 1, right, left)
        there = lax.ppermute(mine, "col", [(half - 1, devices - 1), (half, 0)])
    before = lax.ppermute(right, "col", up)
    after = lax.ppermute(left, "col", down)
    if relayed:
        extra = lax.ppermute(there, "col", [(devices - 1, half), (0, half - 1)])
    return before, after, extra


def masked_rows(upper_band, pattern, first_block, block_total):
    height, width = upper_band.shape
    count = height // BS
    block = first_block + jnp.arange(count, dtype=jnp.int32)
    offset = lax.broadcasted_iota(jnp.int32, (count, BS, width), 2) // BS
    factor = jnp.ones((count, BS, width), F32)
    for d in range(1, KB + 1):
        present = (pattern[:, d - 1] > 0) & (block + d < block_total)
        factor = jnp.where(offset == d, present.astype(F32)[:, None, None], factor)
    return (upper_band.reshape(count, BS, width) * factor).reshape(height, width)


def spread(value, axis, source):
    kept = jnp.where(lax.axis_index(axis) == source, value, 0).astype(value.dtype)
    return lax.psum(kept, axis)


def after(first, *values):
    return lax.optimization_barrier((first, *values))[1:]


def column_panel(panel, width, meanwhile):
    row_devices, col_devices = lax.axis_size("row"), lax.axis_size("col")
    row, col = lax.axis_index("row"), lax.axis_index("col")
    per_row = col_devices // row_devices
    if (row_devices, col_devices) != (4, 8):
        source = col // per_row
        whole = spread(panel, "row", source)
        return lax.dynamic_slice_in_dim(whole, (col - source * per_row) * width, width + G, 0), panel, panel[:G]
    y, x, k = col // 4, (col // 2) % 2, col % 2
    rows = (width + G) // 2
    own = lax.dynamic_slice_in_dim(panel, k * width + y * rows, rows, 0)
    cols = lambda side: [c for c in range(col_devices) if (c // 2) % 2 == side]
    pairs = lambda hops: [
        (r * col_devices + c, t * col_devices + c) for side, r, t in hops for c in cols(side)
    ]
    both = ("row", "col")
    far = lax.ppermute(own, both, pairs([(0, 0, 2), (0, 2, 0), (1, 1, 3), (1, 3, 1)]))
    up = lax.ppermute(own, both, pairs([(0, 0, 1), (0, 2, 3), (1, 1, 2)]))
    down = lax.ppermute(own, both, pairs([(0, 2, 1), (1, 1, 0), (1, 3, 2)]))
    far, up, down = after(meanwhile, far, up, down)
    last = lax.ppermute(far, both, pairs([(0, 2, 3), (1, 1, 0)]))
    at = row - x
    low = jnp.where(at == -1, down, jnp.where(at == 0, own, jnp.where(at == 1, up, jnp.where((at == 2), far, last))))
    high = jnp.where(at == 2, own, jnp.where(at == 1, down, jnp.where(at == 3, up, jnp.where(at == 0, far, last))))
    mine, other = jnp.where(y == 0, low, high), jnp.where(y == 0, high, low)
    got = lax.ppermute(other, "col", [(c, (c + 4) % 8) for c in range(8)])
    parts = [jnp.where(y == 0, mine, got), jnp.where(y == 0, got, mine)]
    return jnp.concatenate(parts, axis=0), last, own


def shards(dens_real, dens_imag, upper_band, pattern):
    height, width = dens_real.shape
    row_blocks = height // BS
    row_devices, col_devices = lax.axis_size("row"), lax.axis_size("col")
    row, col = lax.axis_index("row"), lax.axis_index("col")
    first, total = row * row_blocks, row_blocks * row_devices
    tail = masked_rows(upper_band[-G:], pattern[-KB:], first + row_blocks - KB, total)
    above = lax.ppermute(tail[:, BS:], "row", chain(row_devices, 1))
    masked = masked_rows(upper_band, pattern, first, total)
    panel = jnp.concatenate([jnp.pad(above, ((0, 0), (BS, 0))), masked], axis=0)
    row_band = band_groups(panel, False)
    real, imag = dens_real, dens_imag
    x_real, x_imag = from_left(real, imag, row_band)
    own_panel, landed, own_part = column_panel(panel, width, x_real)
    col_band = band_groups(own_panel, True)

    groups, columns = height // G, width // G
    slot_above, slot_below = 2, groups % 3

    def row_edge(x):
        return jnp.stack(
            [
                x[0, :, slot_above * G : (slot_above + 1) * G],
                x[groups - 1, :, slot_below * G : (slot_below + 1) * G],
            ]
        )

    def col_edge(x):
        return jnp.stack([x[0, :G], x[columns - 1, 2 * G :]])

    row_edge_band = [row_edge(x) for x in row_band]
    col_edge_band = [col_edge(x) for x in col_band]
    half = col_devices // 2
    use = jnp.stack([col == half, col == half - 1]).astype(jnp.int32)

    rim_left = jnp.stack([real[:, :G], imag[:, :G]])
    rim_right = jnp.stack([real[:, -G:], imag[:, -G:]])
    before, behind, _ = swap_col_rims(*after(own_part, rim_left, rim_right), False)
    top, bottom = jnp.stack([real[:G], imag[:G]]), jnp.stack([real[-G:], imag[-G:]])
    above, below = swap_row_rims(*after(landed, top, bottom))
    x_real, x_imag, left = outer_columns(0, real, imag, col_band, before, x_real, x_imag)
    x_real, x_imag, left = row_edges(
        x_real, x_imag, above, below, row_edge_band, 1.0, (left,)
    )
    next_after = lax.ppermute(left, "col", chain(col_devices, -1))
    x_real, x_imag, right = outer_columns(1, real, imag, col_band, behind, x_real, x_imag)
    next_before = lax.ppermute(right, "col", chain(col_devices, 1))
    x_real, x_imag, top, bottom = middle_columns(real, imag, col_band, x_real, x_imag)
    above, below = swap_row_rims(top, bottom)

    scale = -0.5 * STEP_TIME * STEP_TIME
    new_real, new_imag = inner(x_real, x_imag, row_band, col_band, real, imag)
    new_real, new_imag = row_edges(new_real, new_imag, above, below, row_edge_band, scale)
    new_real, new_imag = col_edges(
        new_real, new_imag, (next_before, next_after, None), col_edge_band, scale, use, (0, 1, groups), False
    )
    return new_real, new_imag


def solution(mesh):
    in_specs = (P("row", "col"), P("row", "col"), P("row", None), P("row", None))
    out_specs = (P("row", "col"), P("row", "col"))
    return jax.shard_map(shards, mesh=mesh, in_specs=in_specs, out_specs=out_specs, check_vma=False)
```

time: 706 us -> 280 us (0.40)
  matrix products: 259 us -> 0 us
  other arithmetic: 172 us -> 14.5 us
  Pallas kernels: 0 us -> 149 us
  local copies, waits for them, and re-layouts: 120 us -> 24.5 us
  waiting for transfers between devices: 84.5 us -> 52 us
  starting transfers between devices: 52 us -> 36.8 us
  between operations: 14.9 us -> 1.01 us
    dot_general x8 -> x0, matrix products: 259 us -> none  [the longest x4 132 us: row_product(): jnp.einsum('grw,gwn->grn', dense_groups, windows, precision=HIGHEST_PRECI...]
    pallas_call x0 -> x10, Pallas kernels: none -> 149 us  [the longest x1 46.6 us: inner(): pl.pallas_call(functools.partial(last_kernel, groups), grid=(groups + 1,)...]
    another operation x13 -> x6, other arithmetic: 102 us -> 6.44 us  [the longest x1 4.02 us: shards(): rim_left = jnp.stack([real[:, :G], imag[:, :G]])]
    add x5 -> x0, other arithmetic: 56.2 us -> none  [the longest x1 22.9 us: shards(): new_imag = dens_imag + 0.5 * STEP_TIME * (slope_imag + second_imag)]
    reshape x6 -> x0, local copies, waits for them, and re-layouts: 42.4 us -> none  [the longest x4 37 us: column_product(): return summed.reshape(columns_ext.shape[0], group_count * group_rows)]
    ppermute x17 -> x14, waiting for transfers between devices: 84.5 us -> 52 us  [the longest x1 29.9 us: column_panel(): got = lax.ppermute(other, 'col', [(c, (c + 4) % 8) for c in range(8)])]
    slice x11 -> x8, local copies, waits for them, and re-layouts: 26.9 us -> 4.99 us  [the longest x2 1.98 us: row_edge(): x[0, :, slot_above * G:(slot_above + 1) * G]]
    ppermute x17 -> x14, starting transfers between devices: 52 us -> 36.8 us  [the longest x2 8.58 us: swap_row_rims(): above = lax.ppermute(bottom, 'row', chain(devices, 1))]
  transfers between devices with their start and end apart: 18 -> 14, of which waited for: 6 -> 4; matrix products, arithmetic and copies ran while one was open for 44% -> 9% of each run, Pallas kernels for 0% -> 45%
where the time goes in v1:
time: 280 us; the launch traced here: 278 us
  Pallas kernels  149 us (53%)
  waiting for transfers between devices  52 us (19%)
  starting transfers between devices  36.8 us (13%)
  local copies, waits for them, and re-layouts  24.5 us (9%)
  other arithmetic  14.5 us (5%)
    pallas_call x1, Pallas kernels, inner(): pl.pallas_call(functools.partial(last_kernel, groups), grid=(groups + 1,)...  46.6 us
    ppermute x1, waiting for transfers between devices, column_panel(): got = lax.ppermute(other, 'col', [(c, (c + 4) % 8) for c in range(8)])  29.9 us
    pallas_call x1, Pallas kernels, from_left(): pl.pallas_call(functools.partial(left_kernel, groups), grid=(groups + 1,)...  27.1 us
    pallas_call x1, Pallas kernels, middle_columns(): pl.pallas_call(functools.partial(middle_kernel, groups), grid=(groups,),...  25.1 us
    pallas_call x2, Pallas kernels, outer_columns(): pl.pallas_call(functools.partial(outer_kernel, side), grid=(count,), in_s...  22.9 us
    pallas_call x1, Pallas kernels, col_edges(): pl.pallas_call(functools.partial(col_edge_kernel, scale, relayed, with_ri...  12.8 us
    pallas_call x2, Pallas kernels, row_edges(): pl.pallas_call(functools.partial(row_edge_kernel, scale), grid=(2,), in_s...  12.2 us
    ppermute x2, waiting for transfers between devices, swap_row_rims(): below = lax.ppermute(top, 'row', chain(devices, -1))  10.1 us
  transfers between devices with their start and end apart: 14, of which 4 were waited for; matrix products, arithmetic and copies ran while one was open for 9% of the time, Pallas kernels for 45%

profile of v1, /device:TPU:1, one launch (start us, length us, event | category | flops | bytes accessed | tf_op | source)
XLA Modules:
  0.0 278.3 jit_solution(12459129781771973941)
XLA Ops:
  2.8 4.8 %collective-permute-start = (f32[256,256]{1,0:T(8,128)S(1)}, f32[256,256]{1,0:T(8,128)}, u32[]{:S(2)}, u32[]{:S(2)}) collective-permute-start(f32[256,256]{1,0:T(8,128)S(1)} %slice_multiply_fusion), channel_id=1, source_target_pairs={{0,8},{8,16},{16,24},{1,9},{9,17},{17,25},{2,10},{10,18},{18,26},{... | collective-permute-start | bytes 786440 | tf_op jit(solution)/shard_map/ppermute | solution.py:475
  8.3 4.0 %slice_bitcast_fusion.1 = (f32[1,2048,256]{2,1,0:T(8,128)S(1)}, f32[1,2048,256]{2,1,0:T(8,128)}) fusion(f32[2048,1024]{1,0:T(8,128)} %a_ref.1), kind=kLoop, calls=%fused_computation.10 | loop fusion | bytes 8388608 | tf_op jit(solution)/shard_map/stack | solution.py:504
  13.7 2.4 slice_bitcast_fusion
  16.2 2.4 select_multiply_fusion
  20.0 4.0 %pad_maximum_fusion = (f32[2,2048,256]{2,1,0:T(8,128)}, f32[2,2048,256]{2,1,0:T(8,128)}) fusion(f32[1,2048,256]{2,1,0:T(8,128)S(1)} %copy-done.7, f32[1,2048,256]{2,1,0:T(8,128)S(1)} %copy-done.5, f32[1,2048,256]{2,1,0:T(8,128)S(1)} %copy-done.6, f32[1,2048,256]{2,1,0:T(8,128)S(1)} %get-tuple-element.69), kind=kLoop, calls=%fused_computation.2 | loop fusion | flops 2097152 | bytes 16777216 | tf_op jit(solution)/shard_map/stack | solution.py:503
  25.3 4.0 %collective-permute-start.9 = (f32[2,2048,256]{2,1,0:T(8,128)}, f32[2,2048,256]{2,1,0:T(8,128)}, u32[]{:S(2)}, u32[]{:S(2)}) collective-permute-start(f32[2,2048,256]{2,1,0:T(8,128)} %get-tuple-element.43), channel_id=1, source_target_pairs={{0,1},{1,2},{2,3},{3,4},{4,5},{5,6},{6,7},{8,9},{9,10},{10,11},{11... | collective-permute-start | bytes 12582920 | tf_op jit(solution)/shard_map/ppermute | solution.py:410
  29.3 2.4 collective-permute-start.6
  31.7 3.5 %collective-permute-start.1 = (f32[640,384]{1,0:T(8,128)S(1)}, f32[640,384]{1,0:T(8,128)S(1)}, u32[]{:S(2)}, u32[]{:S(2)}) collective-permute-start(f32[640,384]{1,0:T(8,128)S(1)} %constant_dynamic-slice_fusion), channel_id=1, source_target_pairs={{0,16},{1,17},{4,20},{5,21},{16,0},{17,1},{20,4},{21,5},{10,26},{1... | collective-permute-start | bytes 2949128 | tf_op jit(solution)/shard_map/ppermute | solution.py:454
  37.3 1.9 band_rows.1
  39.2 1.7 copy-done.2
  40.9 1.6 copy-done.3
  42.6 27.1 %from_left.1 = (f32[2048,1024]{1,0:T(8,128)}, f32[2048,1024]{1,0:T(8,128)}) custom-call(f32[2048,1024]{1,0:T(8,128)} %a_ref.1, f32[2048,1024]{1,0:T(8,128)} %b_ref.1, bf16[8,256,768]{2,1,0:T(8,128)(2,1)} %copy-done.2, bf16[8,256,768]{2,1,0:T(8,128)(2,1)} %copy-done.3), custom_call_target="tpu_custom_call" | custom-call | tf_op jit(solution)/shard_map/from_left/pallas_call | solution.py:259
  69.7 8.1 %collective-permute-done.2 = f32[640,384]{1,0:T(8,128)S(1)} collective-permute-done((f32[640,384]{1,0:T(8,128)S(1)}, f32[640,384]{1,0:T(8,128)S(1)}, u32[]{:S(2)}, u32[]{:S(2)}) %collective-permute-start.2) | collective-permute-done | bytes 983072 | tf_op jit(solution)/shard_map/ppermute | solution.py:455
  78.4 1.7 slice_bitcast_fusion.5
  80.1 1.7 slice_bitcast_fusion.4
  81.8 2.3 pad_maximum_fusion.2
  85.1 5.2 %collective-permute-start.7 = (f32[2,256,1024]{2,1,0:T(8,128)}, f32[2,256,1024]{2,1,0:T(8,128)}, u32[]{:S(2)}, u32[]{:S(2)}) collective-permute-start(f32[2,256,1024]{2,1,0:T(8,128)} %get-tuple-element.41), channel_id=1, source_target_pairs={{0,8},{8,16},{16,24},{1,9},{9,17},{17,25},{2,10},{10,18},{18,26},{... | collective-permute-start | bytes 6291464 | tf_op jit(solution)/shard_map/ppermute | solution.py:395
  91.8 2.4 broadcast_select_fusion.2
  96.4 29.9 %collective-permute-done.5 = f32[640,384]{1,0:T(8,128)S(1)} collective-permute-done((f32[640,384]{1,0:T(8,128)S(1)}, f32[640,384]{1,0:T(8,128)S(1)}, u32[]{:S(2)}, u32[]{:S(2)}) %collective-permute-start.5) | collective-permute-done | bytes 983072 | tf_op jit(solution)/shard_map/ppermute | solution.py:463
  129.8 11.4 %outer_columns.2 = (f32[2048,1024]{1,0:T(8,128)}, f32[2048,1024]{1,0:T(8,128)}, f32[2,2048,256]{2,1,0:T(8,128)}) custom-call(f32[2048,1024]{1,0:T(8,128)} %a_ref.1, f32[2048,1024]{1,0:T(8,128)} %b_ref.1, bf16[4,768,256]{2,1,0:T(8,128)(2,1)} %copy-done, bf16[4,768,256]{2,1,0:T(8,128)(2,1)} %copy-done.1, ...), custom_call_target="tpu_custom_call", output_to_operand_aliasing={{0}: (5, {}), {1}: (6, {})} | custom-call | tf_op jit(solution)/shard_map/outer_columns/pallas_call | solution.py:159
  141.2 10.1 %collective-permute-done.8.below_ref = f32[2,256,1024]{2,1,0:T(8,128)} collective-permute-done((f32[2,256,1024]{2,1,0:T(8,128)}, f32[2,256,1024]{2,1,0:T(8,128)}, u32[]{:S(2)}, u32[]{:S(2)}) %collective-permute-start.8) | collective-permute-done | bytes 2097184 | tf_op jit(solution)/shard_map/ppermute | solution.py:396
  151.3 6.6 %row_edges.2 = (f32[2048,1024]{1,0:T(8,128)}, f32[2048,1024]{1,0:T(8,128)}, f32[2,2048,256]{2,1,0:T(8,128)}) custom-call(bf16[2,256,256]{2,1,0:T(8,128)(2,1)S(1)} %pad_maximum_fusion.7.h_ref, bf16[2,256,256]{2,1,0:T(8,128)(2,1)S(1)} %pad_maximum_fusion.8.l_ref, ...), custom_call_target="tpu_custom_call", output_to_operand_aliasing={{0}: (4, {}), {1}: (5, {}), {2}: (6, {})} | custom-call | tf_op jit(solution)/shard_map/row_edges/pallas_call | solution.py:316
  157.9 11.5 %outer_columns.3 = (f32[2048,1024]{1,0:T(8,128)}, f32[2048,1024]{1,0:T(8,128)}, f32[2,2048,256]{2,1,0:T(8,128)}) custom-call(f32[2048,1024]{1,0:T(8,128)} %a_ref.1, f32[2048,1024]{1,0:T(8,128)} %b_ref.1, bf16[4,768,256]{2,1,0:T(8,128)(2,1)} %copy-done, bf16[4,768,256]{2,1,0:T(8,128)(2,1)} %copy-done.1, ...), custom_call_target="tpu_custom_call", output_to_operand_aliasing={{0}: (5, {}), {1}: (6, {})} | custom-call | tf_op jit(solution)/shard_map/outer_columns/pallas_call | solution.py:159
  169.4 5.9 %collective-permute-start.10 = (f32[2,2048,256]{2,1,0:T(8,128)}, f32[2,2048,256]{2,1,0:T(8,128)}, u32[]{:S(2)}, u32[]{:S(2)}) collective-permute-start(f32[2,2048,256]{2,1,0:T(8,128)} %get-tuple-element.50), channel_id=1, source_target_pairs={{0,1},{1,2},{2,3},{3,4},{4,5},{5,6},{6,7},{8,9},{9,10},{10,11},{11... | collective-permute-start | bytes 12582920 | tf_op jit(solution)/shard_map/ppermute | solution.py:514
  175.3 1.9 collective-permute-start.11
  177.2 25.1 %middle_columns.1 = (f32[2048,1024]{1,0:T(8,128)}, f32[2048,1024]{1,0:T(8,128)}, f32[2,256,1024]{2,1,0:T(8,128)}, f32[2,256,1024]{2,1,0:T(8,128)}) custom-call(f32[2048,1024]{1,0:T(8,128)} %a_ref.1, f32[2048,1024]{1,0:T(8,128)} %b_ref.1, bf16[4,768,256]{2,1,0:T(8,128)(2,1)} %copy-done, ...), custom_call_target="tpu_custom_call", output_to_operand_aliasing={{0}: (4, {}), {1}: (5, {})} | custom-call | tf_op jit(solution)/shard_map/middle_columns/pallas_call | solution.py:209
  202.3 3.4 %collective-permute-start.12 = (f32[2,256,1024]{2,1,0:T(8,128)}, f32[2,256,1024]{2,1,0:T(8,128)S(1)}, u32[]{:S(2)}, u32[]{:S(2)}) collective-permute-start(f32[2,256,1024]{2,1,0:T(8,128)} %get-tuple-element.54), channel_id=1, source_target_pairs={{0,8},{8,16},{16,24},{1,9},{9,17},{17,25},{2,10},{10,18},{18,26},{... | collective-permute-start | bytes 6291464 | tf_op jit(solution)/shard_map/ppermute | solution.py:395
  205.7 1.5 collective-permute-start.13
  209.3 46.6 %inner.1 = (f32[2048,1024]{1,0:T(8,128)}, f32[2048,1024]{1,0:T(8,128)}) custom-call(f32[2048,1024]{1,0:T(8,128)} %get-tuple-element.56.p_ref.pf_ref, f32[2048,1024]{1,0:T(8,128)} %get-tuple-element.57.q_ref.qf_ref, bf16[8,256,768]{2,1,0:T(8,128)(2,1)} %copy-done.2, bf16[8,256,768]{2,1,0:T(8,128)(2,1)} %copy-done.3, bf16[4,768,256]{2,1,0:T(8,128)(2,1)} %copy-done, ...), custom_call_target="tpu_custom_call" | custom-call | tf_op jit(solution)/shard_map/inner/pallas_call | solution.py:277
  255.9 5.6 %row_edges.3 = (f32[2048,1024]{1,0:T(8,128)}, f32[2048,1024]{1,0:T(8,128)}) custom-call(bf16[2,256,256]{2,1,0:T(8,128)(2,1)S(1)} %pad_maximum_fusion.7.h_ref, bf16[2,256,256]{2,1,0:T(8,128)(2,1)S(1)} %pad_maximum_fusion.8.l_ref, f32[2,256,1024]{2,1,0:T(8,128)S(1)} %collective-permute-done.12.above_ref, ...), custom_call_target="tpu_custom_call", output_to_operand_aliasing={{0}: (4, {}), {1}: (5, {})} | custom-call | tf_op jit(solution)/shard_map/row_edges/pallas_call | solution.py:316
  261.6 3.9 %collective-permute-done.11.refs_3_ = f32[2,2048,256]{2,1,0:T(8,128)} collective-permute-done((f32[2,2048,256]{2,1,0:T(8,128)}, f32[2,2048,256]{2,1,0:T(8,128)}, u32[]{:S(2)}, u32[]{:S(2)}) %collective-permute-start.11) | collective-permute-done | bytes 4194336 | tf_op jit(solution)/shard_map/ppermute | solution.py:512
  265.5 12.8 %col_edges.1 = (f32[2048,1024]{1,0:T(8,128)}, f32[2048,1024]{1,0:T(8,128)}) custom-call(s32[2]{0:T(128)S(1)} %add_convert_fusion.use_ref, bf16[2,256,256]{2,1,0:T(8,128)(2,1)S(1)} %pad_maximum_fusion.5.refs_0_, bf16[2,256,256]{2,1,0:T(8,128)(2,1)S(1)} %pad_maximum_fusion.6.refs_1_, ...), custom_call_target="tpu_custom_call", output_to_operand_aliasing={{0}: (5, {}), {1}: (6, {})} | custom-call | tf_op jit(solution)/shard_map/col_edges/pallas_call | solution.py:374
  (62 shorter events, 19.9 us)
Async XLA Ops:
  2.8 21.3 %collective-permute-start = (f32[256,256]{1,0:T(8,128)S(1)}, f32[256,256]{1,0:T(8,128)}, u32[]{:S(2)}, u32[]{:S(2)}) collective-permute-start(f32[256,256]{1,0:T(8,128)S(1)} %slice_multiply_fusion), channel_id=1, source_target_pairs={{0,8},{8,16},{16,24},{1,9},{9,17},{17,25},{2,10},{10,18},{18,26},{... | collective-permute-start | bytes 786440 | tf_op jit(solution)/shard_map/ppermute | solution.py:475
  8.3 5.4 %copy-start.4 = (f32[2048,1024]{1,0:T(8,128)S(1)}, f32[2048,1024]{1,0:T(8,128)}, u32[]{:S(2)}) copy-start(f32[2048,1024]{1,0:T(8,128)} %b_ref.1) | copy-start | bytes 25165828
  16.2 2.5 copy-start.5
  16.2 3.2 %copy-start.6 = (f32[1,2048,256]{2,1,0:T(8,128)S(1)}, f32[1,2048,256]{2,1,0:T(8,128)}, u32[]{:S(2)}) copy-start(f32[1,2048,256]{2,1,0:T(8,128)} %get-tuple-element.71) | copy-start | bytes 6291460
  16.2 3.8 %copy-start.7 = (f32[1,2048,256]{2,1,0:T(8,128)S(1)}, f32[1,2048,256]{2,1,0:T(8,128)}, u32[]{:S(2)}) copy-start(f32[1,2048,256]{2,1,0:T(8,128)} %get-tuple-element.72) | copy-start | bytes 6291460
  25.3 104.5 %collective-permute-start.9 = (f32[2,2048,256]{2,1,0:T(8,128)}, f32[2,2048,256]{2,1,0:T(8,128)}, u32[]{:S(2)}, u32[]{:S(2)}) collective-permute-start(f32[2,2048,256]{2,1,0:T(8,128)} %get-tuple-element.43), channel_id=1, source_target_pairs={{0,1},{1,2},{2,3},{3,4},{4,5},{5,6},{6,7},{8,9},{9,10},{10,11},{11... | collective-permute-start | bytes 12582920 | tf_op jit(solution)/shard_map/ppermute | solution.py:410
  29.3 128.6 %collective-permute-start.6 = (f32[2,2048,256]{2,1,0:T(8,128)}, f32[2,2048,256]{2,1,0:T(8,128)}, u32[]{:S(2)}, u32[]{:S(2)}) collective-permute-start(f32[2,2048,256]{2,1,0:T(8,128)} %get-tuple-element.40), channel_id=1, source_target_pairs={{1,0},{2,1},{3,2},{4,3},{5,4},{6,5},{7,6},{9,8},{10,9},{11,10},{12... | collective-permute-start | bytes 12582920 | tf_op jit(solution)/shard_map/ppermute | solution.py:411
  31.7 38.0 %collective-permute-start.1 = (f32[640,384]{1,0:T(8,128)S(1)}, f32[640,384]{1,0:T(8,128)S(1)}, u32[]{:S(2)}, u32[]{:S(2)}) collective-permute-start(f32[640,384]{1,0:T(8,128)S(1)} %constant_dynamic-slice_fusion), channel_id=1, source_target_pairs={{0,16},{1,17},{4,20},{5,21},{16,0},{17,1},{20,4},{21,5},{10,26},{1... | collective-permute-start | bytes 2949128 | tf_op jit(solution)/shard_map/ppermute | solution.py:454
  35.2 42.5 %collective-permute-start.2 = (f32[640,384]{1,0:T(8,128)S(1)}, f32[640,384]{1,0:T(8,128)S(1)}, u32[]{:S(2)}, u32[]{:S(2)}) collective-permute-start(f32[640,384]{1,0:T(8,128)S(1)} %constant_dynamic-slice_fusion), channel_id=1, source_target_pairs={{0,8},{1,9},{4,12},{5,13},{16,24},{17,25},{20,28},{21,29},{10,18},... | collective-permute-start | bytes 2949128 | tf_op jit(solution)/shard_map/ppermute | solution.py:455
  36.5 41.2 %collective-permute-start.3 = (f32[640,384]{1,0:T(8,128)S(1)}, f32[640,384]{1,0:T(8,128)S(1)}, u32[]{:S(2)}, u32[]{:S(2)}) collective-permute-start(f32[640,384]{1,0:T(8,128)S(1)} %constant_dynamic-slice_fusion), channel_id=1, source_target_pairs={{16,8},{17,9},{20,12},{21,13},{10,2},{11,3},{14,6},{15,7},{26,18},... | collective-permute-start | bytes 2949128 | tf_op jit(solution)/shard_map/ppermute | solution.py:456
  39.2 1.7 copy-start.2
  40.9 1.6 copy-start.3
  69.6 12.2 %copy-start.8 = (f32[640,384]{1,0:T(8,128)}, f32[640,384]{1,0:T(8,128)S(1)}, u32[]{:S(2)}) copy-start(f32[640,384]{1,0:T(8,128)S(1)} %collective-permute-done.1) | copy-start | bytes 2949124
  77.7 4.1 %copy-start.9 = (f32[640,384]{1,0:T(8,128)}, f32[640,384]{1,0:T(8,128)S(1)}, u32[]{:S(2)}) copy-start(f32[640,384]{1,0:T(8,128)S(1)} %collective-permute-done.2) | copy-start | bytes 2949124
  77.7 4.1 %copy-start.10 = (f32[640,384]{1,0:T(8,128)}, f32[640,384]{1,0:T(8,128)S(1)}, u32[]{:S(2)}) copy-start(f32[640,384]{1,0:T(8,128)S(1)} %collective-permute-done.3) | copy-start | bytes 2949124
  77.7 6.4 %collective-permute-start.4 = (f32[640,384]{1,0:T(8,128)S(1)}, f32[640,384]{1,0:T(8,128)S(1)}, u32[]{:S(2)}, u32[]{:S(2)}) collective-permute-start(f32[640,384]{1,0:T(8,128)S(1)} %collective-permute-done.1), channel_id=1, source_target_pairs={{16,24},{17,25},{20,28},{21,29},{10,2},{11,3},{14,6},{15,7}} | collective-permute-start | bytes 2949128 | tf_op jit(solution)/shard_map/ppermute | solution.py:458
  84.1 1.0 copy-start.11
  85.1 56.1 %collective-permute-start.7 = (f32[2,256,1024]{2,1,0:T(8,128)}, f32[2,256,1024]{2,1,0:T(8,128)}, u32[]{:S(2)}, u32[]{:S(2)}) collective-permute-start(f32[2,256,1024]{2,1,0:T(8,128)} %get-tuple-element.41), channel_id=1, source_target_pairs={{0,8},{8,16},{16,24},{1,9},{9,17},{17,25},{2,10},{10,18},{18,26},{... | collective-permute-start | bytes 6291464 | tf_op jit(solution)/shard_map/ppermute | solution.py:395
  90.3 61.0 %collective-permute-start.8 = (f32[2,256,1024]{2,1,0:T(8,128)}, f32[2,256,1024]{2,1,0:T(8,128)}, u32[]{:S(2)}, u32[]{:S(2)}) collective-permute-start(f32[2,256,1024]{2,1,0:T(8,128)} %get-tuple-element.42), channel_id=1, source_target_pairs={{8,0},{16,8},{24,16},{9,1},{17,9},{25,17},{10,2},{18,10},{26,18},{... | collective-permute-start | bytes 6291464 | tf_op jit(solution)/shard_map/ppermute | solution.py:396
  94.3 32.0 %collective-permute-start.5 = (f32[640,384]{1,0:T(8,128)S(1)}, f32[640,384]{1,0:T(8,128)S(1)}, u32[]{:S(2)}, u32[]{:S(2)}) collective-permute-start(f32[640,384]{1,0:T(8,128)S(1)} %get-tuple-element.62), channel_id=1, source_target_pairs={{0,4},{1,5},{2,6},{3,7},{4,0},{5,1},{6,2},{7,3},{8,12},{9,13},{10,... | collective-permute-start | bytes 2949128 | tf_op jit(solution)/shard_map/ppermute | solution.py:463
  127.4 1.2 copy-start
  128.6 1.2 copy-start.1
  169.4 92.2 %collective-permute-start.10 = (f32[2,2048,256]{2,1,0:T(8,128)}, f32[2,2048,256]{2,1,0:T(8,128)}, u32[]{:S(2)}, u32[]{:S(2)}) collective-permute-start(f32[2,2048,256]{2,1,0:T(8,128)} %get-tuple-element.50), channel_id=1, source_target_pairs={{0,1},{1,2},{2,3},{3,4},{4,5},{5,6},{6,7},{8,9},{9,10},{10,11},{11... | collective-permute-start | bytes 12582920 | tf_op jit(solution)/shard_map/ppermute | solution.py:514
  175.3 90.2 %collective-permute-start.11 = (f32[2,2048,256]{2,1,0:T(8,128)}, f32[2,2048,256]{2,1,0:T(8,128)}, u32[]{:S(2)}, u32[]{:S(2)}) collective-permute-start(f32[2,2048,256]{2,1,0:T(8,128)} %get-tuple-element.51), channel_id=1, source_target_pairs={{1,0},{2,1},{3,2},{4,3},{5,4},{6,5},{7,6},{9,8},{10,9},{11,10},{12... | collective-permute-start | bytes 12582920 | tf_op jit(solution)/shard_map/ppermute | solution.py:512
  202.3 53.6 %collective-permute-start.12 = (f32[2,256,1024]{2,1,0:T(8,128)}, f32[2,256,1024]{2,1,0:T(8,128)S(1)}, u32[]{:S(2)}, u32[]{:S(2)}) collective-permute-start(f32[2,256,1024]{2,1,0:T(8,128)} %get-tuple-element.54), channel_id=1, source_target_pairs={{0,8},{8,16},{16,24},{1,9},{9,17},{17,25},{2,10},{10,18},{18,26},{... | collective-permute-start | bytes 6291464 | tf_op jit(solution)/shard_map/ppermute | solution.py:395
  205.7 50.2 %collective-permute-start.13 = (f32[2,256,1024]{2,1,0:T(8,128)}, f32[2,256,1024]{2,1,0:T(8,128)}, u32[]{:S(2)}, u32[]{:S(2)}) collective-permute-start(f32[2,256,1024]{2,1,0:T(8,128)} %get-tuple-element.55), channel_id=1, source_target_pairs={{8,0},{16,8},{24,16},{9,1},{17,9},{25,17},{10,2},{18,10},{26,18},{... | collective-permute-start | bytes 6291464 | tf_op jit(solution)/shard_map/ppermute | solution.py:396

commit v2 on v1

--- a/solution.py
+++ b/solution.py
@@ -170,50 +170,45 @@
     )(p, q, *col_band, halo, p_left, q_left)
 
 
-def middle_kernel(groups, p_ref, q_ref, ch_ref, cl_ref, pi_ref, qi_ref,
-                  po_ref, qo_ref, top_ref, bottom_ref, rows):
-    i = pl.program_id(0)
-    for k, x_ref in enumerate((p_ref, q_ref)):
-        rows[k], rows[k + 2] = split(x_ref[...])
-    columns = rows.shape[2] // G
-    outs = ((pi_ref, po_ref), (qi_ref, qo_ref))
-    for n in range(columns):
-        at = slice(n * G, (n + 1) * G)
-        if 0 < n < columns - 1:
-            right = right_product(
-                lambda w: rows[:, :, w].reshape(4 * G, w.stop - w.start), n, columns, ch_ref, cl_ref
-            )
-            for k, (i_ref, o_ref) in enumerate(outs):
-                o_ref[:, at] = i_ref[:, at] - right[k * G : (k + 1) * G]
-        else:
-            for i_ref, o_ref in outs:
-                o_ref[:, at] = i_ref[:, at]
-
-    @pl.when(i == 0)
+def middle_kernel(columns, p_ref, q_ref, ch_ref, cl_ref, pi_ref, qi_ref, po_ref, qo_ref, rows):
+    n = pl.program_id(1)
+    height = p_ref.shape[0]
+
+    @pl.when(n == 0)
     def _():
-        top_ref[0], top_ref[1] = po_ref[...], qo_ref[...]
-
-    @pl.when(i == groups - 1)
-    def _():
-        bottom_ref[0], bottom_ref[1] = po_ref[...], qo_ref[...]
+        for k, x_ref in enumerate((p_ref, q_ref)):
+            rows[k], rows[k + 2] = split(x_ref[...])
+
+    def product(at):
+        window = slice((at - 1) * G, (at + 2) * G)
+        high = rows[:2, :, window].reshape(2 * height, 3 * G)
+        low = rows[2:, :, window].reshape(2 * height, 3 * G)
+        right = three(high, low, ch_ref[at], cl_ref[at])
+        po_ref[...] = pi_ref[...] - right[:height]
+        qo_ref[...] = qi_ref[...] - right[height:]
+
+    for at in range(1, columns - 1):
+        pl.when(n == at - 1)(functools.partial(product, at))
 
 
 def middle_columns(p, q, col_band, p_left, q_left):
     height, width = p.shape
-    groups = height // G
-    tile = pl.BlockSpec((G, width), lambda i: (i, 0))
-    band = pl.BlockSpec(col_band[0].shape, lambda i: (0, 0, 0))
-    rim = pl.BlockSpec((2, G, width), lambda i: (0, 0, 0))
+    columns = width // G
+    if columns <= 2:
+        return p_left, q_left
+    rows = min(height, 2 * G)
+    whole = pl.BlockSpec((rows, width), lambda i, n: (i, 0))
+    band = pl.BlockSpec(col_band[0].shape, lambda i, n: (0, 0, 0))
+    tile = pl.BlockSpec((rows, G), lambda i, n: (i, n + 1))
     out = jax.ShapeDtypeStruct(p.shape, F32)
-    rim_out = jax.ShapeDtypeStruct((2, G, width), F32)
-    return pl.pallas_call(
-        functools.partial(middle_kernel, groups),
-        grid=(groups,),
-        in_specs=[tile, tile, band, band, tile, tile],
-        out_specs=[tile, tile, rim, rim],
-        out_shape=[out, out, rim_out, rim_out],
+    return pl.pallas_call(
+        functools.partial(middle_kernel, columns),
+        grid=(height // rows, columns - 2),
+        in_specs=[whole, whole, band, band, tile, tile],
+        out_specs=[tile, tile],
+        out_shape=[out, out],
         input_output_aliases={4: 0, 5: 1},
-        scratch_shapes=[pltpu.VMEM((4, G, width), BF16)],
+        scratch_shapes=[pltpu.VMEM((4, rows, width), BF16)],
         compiler_params=pltpu.CompilerParams(vmem_limit_bytes=56 << 20),
         cost_estimate=pl.CostEstimate(flops=0, bytes_accessed=0, transcendentals=0),
         name="middle_columns",
@@ -442,7 +437,7 @@
     if (row_devices, col_devices) != (4, 8):
         source = col // per_row
         whole = spread(panel, "row", source)
-        return lax.dynamic_slice_in_dim(whole, (col - source * per_row) * width, width + G, 0), panel, panel[:G]
+        return lax.dynamic_slice_in_dim(whole, (col - source * per_row) * width, width + G, 0), panel
     y, x, k = col // 4, (col // 2) % 2, col % 2
     rows = (width + G) // 2
     own = lax.dynamic_slice_in_dim(panel, k * width + y * rows, rows, 0)
@@ -462,7 +457,7 @@
     mine, other = jnp.where(y == 0, low, high), jnp.where(y == 0, high, low)
     got = lax.ppermute(other, "col", [(c, (c + 4) % 8) for c in range(8)])
     parts = [jnp.where(y == 0, mine, got), jnp.where(y == 0, got, mine)]
-    return jnp.concatenate(parts, axis=0), last, own
+    return jnp.concatenate(parts, axis=0), other
 
 
 def shards(dens_real, dens_imag, upper_band, pattern):
@@ -478,7 +473,7 @@
     row_band = band_groups(panel, False)
     real, imag = dens_real, dens_imag
     x_real, x_imag = from_left(real, imag, row_band)
-    own_panel, landed, own_part = column_panel(panel, width, x_real)
+    own_panel, landed = column_panel(panel, width, x_real)
     col_band = band_groups(own_panel, True)
 
     groups, columns = height // G, width // G
@@ -502,7 +497,7 @@
 
     rim_left = jnp.stack([real[:, :G], imag[:, :G]])
     rim_right = jnp.stack([real[:, -G:], imag[:, -G:]])
-    before, behind, _ = swap_col_rims(*after(own_part, rim_left, rim_right), False)
+    before, behind, _ = swap_col_rims(rim_left, rim_right, False)
     top, bottom = jnp.stack([real[:G], imag[:G]]), jnp.stack([real[-G:], imag[-G:]])
     above, below = swap_row_rims(*after(landed, top, bottom))
     x_real, x_imag, left = outer_columns(0, real, imag, col_band, before, x_real, x_imag)
@@ -512,7 +507,8 @@
     next_after = lax.ppermute(left, "col", chain(col_devices, -1))
     x_real, x_imag, right = outer_columns(1, real, imag, col_band, behind, x_real, x_imag)
     next_before = lax.ppermute(right, "col", chain(col_devices, 1))
-    x_real, x_imag, top, bottom = middle_columns(real, imag, col_band, x_real, x_imag)
+    x_real, x_imag = middle_columns(real, imag, col_band, x_real, x_imag)
+    top, bottom = jnp.stack([x_real[:G], x_imag[:G]]), jnp.stack([x_real[-G:], x_imag[-G:]])
     above, below = swap_row_rims(top, bottom)
 
     scale = -0.5 * STEP_TIME * STEP_TIME

time: 280 us -> 274 us (0.979)
  waiting for transfers between devices: 52 us -> 39.7 us
  starting transfers between devices: 36.8 us -> 45.4 us
  other arithmetic: 14.5 us -> 18.3 us
  Pallas kernels: 149 us -> 146 us
    ppermute x1, waiting for transfers between devices: 8.05 us -> 0.53 us  [column_panel(): up = lax.ppermute(own, both, pairs([(0, 0, 1), (0, 2, 3), (1, 1, 2)]))]
    ppermute x1, waiting for transfers between devices: 29.9 us -> 22.8 us  [column_panel(): got = lax.ppermute(other, 'col', [(c, (c + 4) % 8) for c in range(8)])]
    another operation x0 -> x3, other arithmetic: none -> 5.42 us  [the longest x1 2.4 us: shards(): rim_right = jnp.stack([real[:, -G:], imag[:, -G:]])]
    ppermute x2, waiting for transfers between devices: 10.1 us -> 15.3 us  [swap_row_rims(): below = lax.ppermute(top, 'row', chain(devices, -1))]
    ppermute x1, waiting for transfers between devices: 3.9 us -> 0.01 us  [shards(): next_after = lax.ppermute(left, 'col', chain(col_devices, -1))]
    unnamed x24 -> x16, local copies, waits for them, and re-layouts: 9.52 us -> 5.7 us
    another operation x0 -> x2, local copies, waits for them, and re-layouts: none -> 3.35 us  [shards(): jnp.stack([x_real[:G], x_imag[:G]])]
    ppermute x1, starting transfers between devices: 5.9 us -> 9.14 us  [shards(): next_before = lax.ppermute(right, 'col', chain(col_devices, 1))]
  transfers between devices with their start and end apart: 14 -> 14, of which waited for: 4 -> 4; matrix products, arithmetic and copies ran while one was open for 9% -> 12% of each run, Pallas kernels for 45% -> 44%
where the time goes in v2:
time: 274 us
  Pallas kernels  146 us (53%)
  starting transfers between devices  45.4 us (17%)
  waiting for transfers between devices  39.7 us (14%)
  local copies, waits for them, and re-layouts  23.6 us (9%)
  other arithmetic  18.3 us (7%)
    pallas_call x1, Pallas kernels, inner(): pl.pallas_call(functools.partial(last_kernel, groups), grid=(groups + 1,)...  46.6 us
    pallas_call x1, Pallas kernels, from_left(): pl.pallas_call(functools.partial(left_kernel, groups), grid=(groups + 1,)...  27.1 us
    pallas_call x2, Pallas kernels, outer_columns(): pl.pallas_call(functools.partial(outer_kernel, side), grid=(count,), in_s...  22.9 us
    ppermute x1, waiting for transfers between devices, column_panel(): got = lax.ppermute(other, 'col', [(c, (c + 4) % 8) for c in range(8)])  22.8 us
    pallas_call x1, Pallas kernels, middle_columns(): pl.pallas_call(functools.partial(middle_kernel, columns), grid=(height //...  22.6 us
    ppermute x2, waiting for transfers between devices, swap_row_rims(): below = lax.ppermute(top, 'row', chain(devices, -1))  15.3 us
    pallas_call x1, Pallas kernels, col_edges(): pl.pallas_call(functools.partial(col_edge_kernel, scale, relayed, with_ri...  12.8 us
    pallas_call x2, Pallas kernels, row_edges(): pl.pallas_call(functools.partial(row_edge_kernel, scale), grid=(2,), in_s...  10.8 us
  transfers between devices with their start and end apart: 14, of which 4 were waited for; matrix products, arithmetic and copies ran while one was open for 12% of the time, Pallas kernels for 44%

profile of v2, /device:TPU:1, one launch (start us, length us, event | category | flops | bytes accessed | tf_op | source)
XLA Modules:
  0.0 273.6 jit_solution(11055336234545774353)
XLA Ops:
  2.8 4.8 %collective-permute-start = (f32[256,256]{1,0:T(8,128)S(1)}, f32[256,256]{1,0:T(8,128)}, u32[]{:S(2)}, u32[]{:S(2)}) collective-permute-start(f32[256,256]{1,0:T(8,128)S(1)} %slice_multiply_fusion), channel_id=1, source_target_pairs={{0,8},{8,16},{16,24},{1,9},{9,17},{17,25},{2,10},{10,18},{18,26},{... | collective-permute-start | bytes 786440 | tf_op jit(solution)/shard_map/ppermute | solution.py:470
  7.5 6.0 %slice_bitcast_fusion = (f32[1,2048,256]{2,1,0:T(8,128)S(1)}, f32[1,2048,256]{2,1,0:T(8,128)}, f32[1,2048,256]{2,1,0:T(8,128)}, f32[1,2048,256]{2,1,0:T(8,128)S(1)}) fusion(f32[2048,1024]{1,0:T(8,128)} %b_ref.1, f32[2048,1024]{1,0:T(8,128)} %a_ref.1), kind=kLoop, calls=%fused_computation.11 | loop fusion | bytes 16777216 | tf_op jit(solution)/shard_map/stack | solution.py:499
  13.6 2.4 pad_maximum_fusion.1
  16.0 4.1 %collective-permute-start.9 = (f32[2,2048,256]{2,1,0:T(8,128)}, f32[2,2048,256]{2,1,0:T(8,128)}, u32[]{:S(2)}, u32[]{:S(2)}) collective-permute-start(f32[2,2048,256]{2,1,0:T(8,128)} %pad_maximum_fusion.1), channel_id=1, source_target_pairs={{0,1},{1,2},{2,3},{3,4},{4,5},{5,6},{6,7},{8,9},{9,10},{10,11},{11... | collective-permute-start | bytes 12582920 | tf_op jit(solution)/shard_map/ppermute | solution.py:405
  20.2 2.0 select_multiply_fusion
  22.2 2.3 select_maximum_fusion.u_ref
  24.6 3.5 %collective-permute-start.1 = (f32[640,384]{1,0:T(8,128)S(1)}, f32[640,384]{1,0:T(8,128)}, u32[]{:S(2)}, u32[]{:S(2)}) collective-permute-start(f32[640,384]{1,0:T(8,128)S(1)} %constant_dynamic-slice_fusion), channel_id=1, source_target_pairs={{0,16},{1,17},{4,20},{5,21},{16,0},{17,1},{20,4},{21,5},{10,26},{1... | collective-permute-start | bytes 2949128 | tf_op jit(solution)/shard_map/ppermute | solution.py:449
  28.1 2.3 collective-permute-start.2
  32.0 2.3 pad_maximum_fusion
  34.3 2.6 collective-permute-start.6
  36.9 1.9 band_rows.1
  38.9 1.7 copy-done.2
  42.2 27.1 %from_left.1 = (f32[2048,1024]{1,0:T(8,128)}, f32[2048,1024]{1,0:T(8,128)}) custom-call(f32[2048,1024]{1,0:T(8,128)} %a_ref.1, f32[2048,1024]{1,0:T(8,128)} %b_ref.1, bf16[8,256,768]{2,1,0:T(8,128)(2,1)} %copy-done.2, bf16[8,256,768]{2,1,0:T(8,128)(2,1)} %copy-done.3), custom_call_target="tpu_custom_call" | custom-call | tf_op jit(solution)/shard_map/from_left/pallas_call | solution.py:254
  71.5 1.7 slice_bitcast_fusion.9
  73.1 1.7 slice_bitcast_fusion.8
  74.8 2.4 pad_maximum_fusion.2
  77.2 2.4 broadcast_select_fusion.2
  79.6 4.3 %collective-permute-start.7 = (f32[2,256,1024]{2,1,0:T(8,128)}, f32[2,256,1024]{2,1,0:T(8,128)S(1)}, u32[]{:S(2)}, u32[]{:S(2)}) collective-permute-start(f32[2,256,1024]{2,1,0:T(8,128)} %get-tuple-element.36), channel_id=1, source_target_pairs={{0,8},{8,16},{16,24},{1,9},{9,17},{17,25},{2,10},{10,18},{18,26},{... | collective-permute-start | bytes 6291464 | tf_op jit(solution)/shard_map/ppermute | solution.py:390
  88.9 22.8 %collective-permute-done.5 = f32[640,384]{1,0:T(8,128)S(1)} collective-permute-done((f32[640,384]{1,0:T(8,128)S(1)}, f32[640,384]{1,0:T(8,128)S(1)}, u32[]{:S(2)}, u32[]{:S(2)}) %collective-permute-start.5) | collective-permute-done | bytes 983072 | tf_op jit(solution)/shard_map/ppermute | solution.py:458
  115.3 11.4 %outer_columns.2 = (f32[2048,1024]{1,0:T(8,128)}, f32[2048,1024]{1,0:T(8,128)}, f32[2,2048,256]{2,1,0:T(8,128)}) custom-call(f32[2048,1024]{1,0:T(8,128)} %a_ref.1, f32[2048,1024]{1,0:T(8,128)} %b_ref.1, bf16[4,768,256]{2,1,0:T(8,128)(2,1)} %copy-done, bf16[4,768,256]{2,1,0:T(8,128)(2,1)} %copy-done.1, ...), custom_call_target="tpu_custom_call", output_to_operand_aliasing={{0}: (5, {}), {1}: (6, {})} | custom-call | tf_op jit(solution)/shard_map/outer_columns/pallas_call | solution.py:159
  127.7 15.3 %collective-permute-done.8.below_ref = f32[2,256,1024]{2,1,0:T(8,128)S(1)} collective-permute-done((f32[2,256,1024]{2,1,0:T(8,128)}, f32[2,256,1024]{2,1,0:T(8,128)S(1)}, u32[]{:S(2)}, u32[]{:S(2)}) %collective-permute-start.8) | collective-permute-done | bytes 2097184 | tf_op jit(solution)/shard_map/ppermute | solution.py:391
  143.0 5.2 %row_edges.2 = (f32[2048,1024]{1,0:T(8,128)}, f32[2048,1024]{1,0:T(8,128)}, f32[2,2048,256]{2,1,0:T(8,128)}) custom-call(bf16[2,256,256]{2,1,0:T(8,128)(2,1)S(1)} %pad_maximum_fusion.9.h_ref, bf16[2,256,256]{2,1,0:T(8,128)(2,1)S(1)} %pad_maximum_fusion.10.l_ref, ...), custom_call_target="tpu_custom_call", output_to_operand_aliasing={{0}: (4, {}), {1}: (5, {}), {2}: (6, {})} | custom-call | tf_op jit(solution)/shard_map/row_edges/pallas_call | solution.py:311
  148.2 11.5 %outer_columns.3 = (f32[2048,1024]{1,0:T(8,128)}, f32[2048,1024]{1,0:T(8,128)}, f32[2,2048,256]{2,1,0:T(8,128)}) custom-call(f32[2048,1024]{1,0:T(8,128)} %a_ref.1, f32[2048,1024]{1,0:T(8,128)} %b_ref.1, bf16[4,768,256]{2,1,0:T(8,128)(2,1)} %copy-done, bf16[4,768,256]{2,1,0:T(8,128)(2,1)} %copy-done.1, ...), custom_call_target="tpu_custom_call", output_to_operand_aliasing={{0}: (5, {}), {1}: (6, {})} | custom-call | tf_op jit(solution)/shard_map/outer_columns/pallas_call | solution.py:159
  159.7 9.1 %collective-permute-start.10 = (f32[2,2048,256]{2,1,0:T(8,128)}, f32[2,2048,256]{2,1,0:T(8,128)}, u32[]{:S(2)}, u32[]{:S(2)}) collective-permute-start(f32[2,2048,256]{2,1,0:T(8,128)} %get-tuple-element.44), channel_id=1, source_target_pairs={{0,1},{1,2},{2,3},{3,4},{4,5},{5,6},{6,7},{8,9},{9,10},{10,11},{11... | collective-permute-start | bytes 12582920 | tf_op jit(solution)/shard_map/ppermute | solution.py:509
  168.8 1.9 collective-permute-start.11
  170.8 22.6 %middle_columns.1 = (f32[2048,1024]{1,0:T(8,128)}, f32[2048,1024]{1,0:T(8,128)}) custom-call(f32[2048,1024]{1,0:T(8,128)} %a_ref.1, f32[2048,1024]{1,0:T(8,128)} %b_ref.1, bf16[4,768,256]{2,1,0:T(8,128)(2,1)} %copy-done, bf16[4,768,256]{2,1,0:T(8,128)(2,1)} %copy-done.1, ...), custom_call_target="tpu_custom_call", output_to_operand_aliasing={{0}: (4, {}), {1}: (5, {})} | custom-call | tf_op jit(solution)/shard_map/middle_columns/pallas_call | solution.py:204
  193.4 1.7 slice_bitcast_fusion.5
  195.1 1.7 slice_bitcast_fusion.4
  201.1 5.3 %collective-permute-start.12 = (f32[2,256,1024]{2,1,0:T(8,128)}, f32[2,256,1024]{2,1,0:T(8,128)}, u32[]{:S(2)}, u32[]{:S(2)}) collective-permute-start(f32[2,256,1024]{2,1,0:T(8,128)} %pad_maximum_fusion.4), channel_id=1, source_target_pairs={{0,8},{8,16},{16,24},{1,9},{9,17},{17,25},{2,10},{10,18},{18,26},{... | collective-permute-start | bytes 6291464 | tf_op jit(solution)/shard_map/ppermute | solution.py:390
  208.5 46.6 %inner.1 = (f32[2048,1024]{1,0:T(8,128)}, f32[2048,1024]{1,0:T(8,128)}) custom-call(f32[2048,1024]{1,0:T(8,128)} %get-tuple-element.48.p_ref.pf_ref, f32[2048,1024]{1,0:T(8,128)} %get-tuple-element.49.q_ref.qf_ref, bf16[8,256,768]{2,1,0:T(8,128)(2,1)} %copy-done.2, bf16[8,256,768]{2,1,0:T(8,128)(2,1)} %copy-done.3, bf16[4,768,256]{2,1,0:T(8,128)(2,1)} %copy-done, ...), custom_call_target="tpu_custom_call" | custom-call | tf_op jit(solution)/shard_map/inner/pallas_call | solution.py:272
  255.1 5.6 %row_edges.3 = (f32[2048,1024]{1,0:T(8,128)}, f32[2048,1024]{1,0:T(8,128)}) custom-call(bf16[2,256,256]{2,1,0:T(8,128)(2,1)S(1)} %pad_maximum_fusion.9.h_ref, bf16[2,256,256]{2,1,0:T(8,128)(2,1)S(1)} %pad_maximum_fusion.10.l_ref, f32[2,256,1024]{2,1,0:T(8,128)} %collective-permute-done.12.above_ref, ...), custom_call_target="tpu_custom_call", output_to_operand_aliasing={{0}: (4, {}), {1}: (5, {})} | custom-call | tf_op jit(solution)/shard_map/row_edges/pallas_call | solution.py:311
  260.8 12.8 %col_edges.1 = (f32[2048,1024]{1,0:T(8,128)}, f32[2048,1024]{1,0:T(8,128)}) custom-call(s32[2]{0:T(128)S(1)} %add_convert_fusion.use_ref, bf16[2,256,256]{2,1,0:T(8,128)(2,1)S(1)} %pad_maximum_fusion.7.refs_0_, bf16[2,256,256]{2,1,0:T(8,128)(2,1)S(1)} %pad_maximum_fusion.8.refs_1_, ...), custom_call_target="tpu_custom_call", output_to_operand_aliasing={{0}: (5, {}), {1}: (6, {})} | custom-call | tf_op jit(solution)/shard_map/col_edges/pallas_call | solution.py:369
  (58 shorter events, 23.5 us)
Async XLA Ops:
  2.8 19.4 %collective-permute-start = (f32[256,256]{1,0:T(8,128)S(1)}, f32[256,256]{1,0:T(8,128)}, u32[]{:S(2)}, u32[]{:S(2)}) collective-permute-start(f32[256,256]{1,0:T(8,128)S(1)} %slice_multiply_fusion), channel_id=1, source_target_pairs={{0,8},{8,16},{16,24},{1,9},{9,17},{17,25},{2,10},{10,18},{18,26},{... | collective-permute-start | bytes 786440 | tf_op jit(solution)/shard_map/ppermute | solution.py:470
  13.6 6.5 %copy-start.7 = (s32[16,2]{0,1:T(2,128)S(1)}, s32[16,2]{0,1:T(2,128)}, u32[]{:S(2)}) copy-start(s32[16,2]{0,1:T(2,128)} %param.7) | copy-start | bytes 388
  13.6 6.6 %copy-start.6 = (f32[2048,384]{1,0:T(8,128)S(1)}, f32[2048,384]{1,0:T(8,128)}, u32[]{:S(2)}) copy-start(f32[2048,384]{1,0:T(8,128)} %param.6) | copy-start | bytes 9437188
  16.0 99.3 %collective-permute-start.9 = (f32[2,2048,256]{2,1,0:T(8,128)}, f32[2,2048,256]{2,1,0:T(8,128)}, u32[]{:S(2)}, u32[]{:S(2)}) collective-permute-start(f32[2,2048,256]{2,1,0:T(8,128)} %pad_maximum_fusion.1), channel_id=1, source_target_pairs={{0,1},{1,2},{2,3},{3,4},{4,5},{5,6},{6,7},{8,9},{9,10},{10,11},{11... | collective-permute-start | bytes 12582920 | tf_op jit(solution)/shard_map/ppermute | solution.py:405
  22.2 9.8 %copy-start.4 = (f32[1,2048,256]{2,1,0:T(8,128)S(1)}, f32[1,2048,256]{2,1,0:T(8,128)}, u32[]{:S(2)}) copy-start(f32[1,2048,256]{2,1,0:T(8,128)} %get-tuple-element.64) | copy-start | bytes 6291460
  22.2 9.8 %copy-start.5 = (f32[1,2048,256]{2,1,0:T(8,128)S(1)}, f32[1,2048,256]{2,1,0:T(8,128)}, u32[]{:S(2)}) copy-start(f32[1,2048,256]{2,1,0:T(8,128)} %get-tuple-element.89) | copy-start | bytes 6291460
  24.6 44.7 %collective-permute-start.1 = (f32[640,384]{1,0:T(8,128)S(1)}, f32[640,384]{1,0:T(8,128)}, u32[]{:S(2)}, u32[]{:S(2)}) collective-permute-start(f32[640,384]{1,0:T(8,128)S(1)} %constant_dynamic-slice_fusion), channel_id=1, source_target_pairs={{0,16},{1,17},{4,20},{5,21},{16,0},{17,1},{20,4},{21,5},{10,26},{1... | collective-permute-start | bytes 2949128 | tf_op jit(solution)/shard_map/ppermute | solution.py:449
  28.1 41.7 %collective-permute-start.2 = (f32[640,384]{1,0:T(8,128)S(1)}, f32[640,384]{1,0:T(8,128)}, u32[]{:S(2)}, u32[]{:S(2)}) collective-permute-start(f32[640,384]{1,0:T(8,128)S(1)} %constant_dynamic-slice_fusion), channel_id=1, source_target_pairs={{0,8},{1,9},{4,12},{5,13},{16,24},{17,25},{20,28},{21,29},{10,18},... | collective-permute-start | bytes 2949128 | tf_op jit(solution)/shard_map/ppermute | solution.py:450
  30.4 39.4 %collective-permute-start.3 = (f32[640,384]{1,0:T(8,128)S(1)}, f32[640,384]{1,0:T(8,128)}, u32[]{:S(2)}, u32[]{:S(2)}) collective-permute-start(f32[640,384]{1,0:T(8,128)S(1)} %constant_dynamic-slice_fusion), channel_id=1, source_target_pairs={{16,8},{17,9},{20,12},{21,13},{10,2},{11,3},{14,6},{15,7},{26,18},... | collective-permute-start | bytes 2949128 | tf_op jit(solution)/shard_map/ppermute | solution.py:451
  34.3 114.0 %collective-permute-start.6 = (f32[2,2048,256]{2,1,0:T(8,128)}, f32[2,2048,256]{2,1,0:T(8,128)}, u32[]{:S(2)}, u32[]{:S(2)}) collective-permute-start(f32[2,2048,256]{2,1,0:T(8,128)} %pad_maximum_fusion), channel_id=1, source_target_pairs={{1,0},{2,1},{3,2},{4,3},{5,4},{6,5},{7,6},{9,8},{10,9},{11,10},{12... | collective-permute-start | bytes 12582920 | tf_op jit(solution)/shard_map/ppermute | solution.py:406
  38.9 1.7 copy-start.2
  40.6 1.6 copy-start.3
  69.8 7.4 %collective-permute-start.4 = (f32[640,384]{1,0:T(8,128)}, f32[640,384]{1,0:T(8,128)}, u32[]{:S(2)}, u32[]{:S(2)}) collective-permute-start(f32[640,384]{1,0:T(8,128)} %collective-permute-done.1), channel_id=1, source_target_pairs={{16,24},{17,25},{20,28},{21,29},{10,2},{11,3},{14,6},{15,7}} | collective-permute-start | bytes 2949128 | tf_op jit(solution)/shard_map/ppermute | solution.py:453
  79.6 48.1 %collective-permute-start.7 = (f32[2,256,1024]{2,1,0:T(8,128)}, f32[2,256,1024]{2,1,0:T(8,128)S(1)}, u32[]{:S(2)}, u32[]{:S(2)}) collective-permute-start(f32[2,256,1024]{2,1,0:T(8,128)} %get-tuple-element.36), channel_id=1, source_target_pairs={{0,8},{8,16},{16,24},{1,9},{9,17},{17,25},{2,10},{10,18},{18,26},{... | collective-permute-start | bytes 6291464 | tf_op jit(solution)/shard_map/ppermute | solution.py:390
  83.9 59.1 %collective-permute-start.8 = (f32[2,256,1024]{2,1,0:T(8,128)}, f32[2,256,1024]{2,1,0:T(8,128)S(1)}, u32[]{:S(2)}, u32[]{:S(2)}) collective-permute-start(f32[2,256,1024]{2,1,0:T(8,128)} %get-tuple-element.37), channel_id=1, source_target_pairs={{8,0},{16,8},{24,16},{9,1},{17,9},{25,17},{10,2},{18,10},{26,18},{... | collective-permute-start | bytes 6291464 | tf_op jit(solution)/shard_map/ppermute | solution.py:391
  85.2 26.5 %collective-permute-start.5 = (f32[640,384]{1,0:T(8,128)S(1)}, f32[640,384]{1,0:T(8,128)S(1)}, u32[]{:S(2)}, u32[]{:S(2)}) collective-permute-start(f32[640,384]{1,0:T(8,128)S(1)} %get-tuple-element.54), channel_id=1, source_target_pairs={{0,4},{1,5},{2,6},{3,7},{4,0},{5,1},{6,2},{7,3},{8,12},{9,13},{10,... | collective-permute-start | bytes 2949128 | tf_op jit(solution)/shard_map/ppermute | solution.py:458
  112.9 1.2 copy-start
  114.1 1.2 copy-start.1
  159.7 101.1 %collective-permute-start.10 = (f32[2,2048,256]{2,1,0:T(8,128)}, f32[2,2048,256]{2,1,0:T(8,128)}, u32[]{:S(2)}, u32[]{:S(2)}) collective-permute-start(f32[2,2048,256]{2,1,0:T(8,128)} %get-tuple-element.44), channel_id=1, source_target_pairs={{0,1},{1,2},{2,3},{3,4},{4,5},{5,6},{6,7},{8,9},{9,10},{10,11},{11... | collective-permute-start | bytes 12582920 | tf_op jit(solution)/shard_map/ppermute | solution.py:509
  168.8 91.9 %collective-permute-start.11 = (f32[2,2048,256]{2,1,0:T(8,128)}, f32[2,2048,256]{2,1,0:T(8,128)}, u32[]{:S(2)}, u32[]{:S(2)}) collective-permute-start(f32[2,2048,256]{2,1,0:T(8,128)} %get-tuple-element.45), channel_id=1, source_target_pairs={{1,0},{2,1},{3,2},{4,3},{5,4},{6,5},{7,6},{9,8},{10,9},{11,10},{12... | collective-permute-start | bytes 12582920 | tf_op jit(solution)/shard_map/ppermute | solution.py:507
  198.3 56.9 %collective-permute-start.13 = (f32[2,256,1024]{2,1,0:T(8,128)}, f32[2,256,1024]{2,1,0:T(8,128)S(1)}, u32[]{:S(2)}, u32[]{:S(2)}) collective-permute-start(f32[2,256,1024]{2,1,0:T(8,128)} %pad_maximum_fusion.5), channel_id=1, source_target_pairs={{8,0},{16,8},{24,16},{9,1},{17,9},{25,17},{10,2},{18,10},{26,18},{... | collective-permute-start | bytes 6291464 | tf_op jit(solution)/shard_map/ppermute | solution.py:391
  201.1 54.1 %collective-permute-start.12 = (f32[2,256,1024]{2,1,0:T(8,128)}, f32[2,256,1024]{2,1,0:T(8,128)}, u32[]{:S(2)}, u32[]{:S(2)}) collective-permute-start(f32[2,256,1024]{2,1,0:T(8,128)} %pad_maximum_fusion.4), channel_id=1, source_target_pairs={{0,8},{8,16},{16,24},{1,9},{9,17},{17,25},{2,10},{10,18},{18,26},{... | collective-permute-start | bytes 6291464 | tf_op jit(solution)/shard_map/ppermute | solution.py:390

commit v3 on v2

--- a/solution.py
+++ b/solution.py
@@ -113,18 +113,30 @@
     return three(rows[: 2 * G], rows[2 * G :], ch_ref[n, band, :], cl_ref[n, band, :])
 
 
-def left_kernel(groups, p_ref, q_ref, hh_ref, hl_ref, po_ref, qo_ref, *ring):
+def left_kernel(groups, p_ref, hh_ref, hl_ref, po_ref, high, low):
     t = pl.program_id(0)
-    load_ring(t, groups, p_ref, q_ref, ring)
+    slot = lax.rem(t, 3)
+
+    @pl.when(t == 0)
+    def _():
+        for ref in (high, low):
+            ref[2] = jnp.zeros(ref.shape[1:], BF16)
+
+    @pl.when(t < groups)
+    def _():
+        high[slot], low[slot] = split(p_ref[...])
+
+    @pl.when(t == groups)
+    def _():
+        for ref in (high, low):
+            ref[slot] = jnp.zeros(ref.shape[1:], BF16)
 
     @pl.when(t > 0)
     def _():
-        ph, pl_, qh, ql = ring
         both = jnp.concatenate([hh_ref[0], hl_ref[0]], axis=0)
-        for n in range(ph.shape[2] // G):
+        for n in range(high.shape[2] // G):
             at = slice(n * G, (n + 1) * G)
-            po_ref[:, at] = left_product(both, ph, pl_, at)
-            qo_ref[:, at] = left_product(both, qh, ql, at)
+            po_ref[:, at] = left_product(both, high, low, at)
 
 
 def outer_kernel(side, p_ref, q_ref, h_ref, l_ref, halo_ref, pi_ref, qi_ref,
@@ -247,21 +259,20 @@
     return ahead, behind, band, [pltpu.VMEM((3, G, width), BF16)] * 4
 
 
-def from_left(p, q, row_band):
+def from_left(p, row_band):
     groups = p.shape[0] // G
     ahead, behind, band, ring = ring_specs(p, groups)
-    out = jax.ShapeDtypeStruct(p.shape, F32)
     return pl.pallas_call(
         functools.partial(left_kernel, groups),
         grid=(groups + 1,),
-        in_specs=[ahead, ahead, band, band],
-        out_specs=[behind, behind],
-        out_shape=[out, out],
-        scratch_shapes=ring,
+        in_specs=[ahead, band, band],
+        out_specs=behind,
+        out_shape=jax.ShapeDtypeStruct(p.shape, F32),
+        scratch_shapes=ring[:2],
         compiler_params=pltpu.CompilerParams(vmem_limit_bytes=56 << 20),
         cost_estimate=pl.CostEstimate(flops=0, bytes_accessed=0, transcendentals=0),
         name="from_left",
-    )(p, q, *row_band)
+    )(p, *row_band)
 
 
 def inner(p, q, row_band, col_band, a, b):
@@ -430,17 +441,17 @@
     return lax.optimization_barrier((first, *values))[1:]
 
 
-def column_panel(panel, width, meanwhile):
+def column_panel(panel, width, meanwhile, ahead):
     row_devices, col_devices = lax.axis_size("row"), lax.axis_size("col")
     row, col = lax.axis_index("row"), lax.axis_index("col")
     per_row = col_devices // row_devices
     if (row_devices, col_devices) != (4, 8):
         source = col // per_row
         whole = spread(panel, "row", source)
-        return lax.dynamic_slice_in_dim(whole, (col - source * per_row) * width, width + G, 0), panel
+        return lax.dynamic_slice_in_dim(whole, (col - source * per_row) * width, width + G, 0), panel, panel[:G], panel
     y, x, k = col // 4, (col // 2) % 2, col % 2
     rows = (width + G) // 2
-    own = lax.dynamic_slice_in_dim(panel, k * width + y * rows, rows, 0)
+    (own,) = after(ahead, lax.dynamic_slice_in_dim(panel, k * width + y * rows, rows, 0))
     cols = lambda side: [c for c in range(col_devices) if (c // 2) % 2 == side]
     pairs = lambda hops: [
         (r * col_devices + c, t * col_devices + c) for side, r, t in hops for c in cols(side)
@@ -457,7 +468,7 @@
     mine, other = jnp.where(y == 0, low, high), jnp.where(y == 0, high, low)
     got = lax.ppermute(other, "col", [(c, (c + 4) % 8) for c in range(8)])
     parts = [jnp.where(y == 0, mine, got), jnp.where(y == 0, got, mine)]
-    return jnp.concatenate(parts, axis=0), other
+    return jnp.concatenate(parts, axis=0), other, own, far
 
 
 def shards(dens_real, dens_imag, upper_band, pattern):
@@ -472,8 +483,11 @@
     panel = jnp.concatenate([jnp.pad(above, ((0, 0), (BS, 0))), masked], axis=0)
     row_band = band_groups(panel, False)
     real, imag = dens_real, dens_imag
-    x_real, x_imag = from_left(real, imag, row_band)
-    own_panel, landed = column_panel(panel, width, x_real)
+    x_real = from_left(real, row_band)
+    rim_left = jnp.stack([x[:, :G] for x in (real, imag)])
+    rim_right = jnp.stack([x[:, -G:] for x in (real, imag)])
+    own_panel, landed, own_part, began = column_panel(panel, width, x_real, (rim_left, rim_right))
+    x_imag = from_left(*after(began, imag), row_band)
     col_band = band_groups(own_panel, True)
 
     groups, columns = height // G, width // G
@@ -495,8 +509,6 @@
     half = col_devices // 2
     use = jnp.stack([col == half, col == half - 1]).astype(jnp.int32)
 
-    rim_left = jnp.stack([real[:, :G], imag[:, :G]])
-    rim_right = jnp.stack([real[:, -G:], imag[:, -G:]])
     before, behind, _ = swap_col_rims(rim_left, rim_right, False)
     top, bottom = jnp.stack([real[:G], imag[:G]]), jnp.stack([real[-G:], imag[-G:]])
     above, below = swap_row_rims(*after(landed, top, bottom))

time: 274 us -> 273 us (level)
  waiting for transfers between devices: 39.7 us -> 32.4 us
  Pallas kernels: 146 us -> 150 us
    ppermute x2, waiting for transfers between devices: 15.3 us -> 0.01 us  [swap_row_rims(): below = lax.ppermute(top, 'row', chain(devices, -1))]
    ppermute x1, waiting for transfers between devices: 0.53 us -> 11.3 us  [column_panel(): up = lax.ppermute(own, both, pairs([(0, 0, 1), (0, 2, 3), (1, 1, 2)]))]
    pallas_call x1 -> x2, Pallas kernels: 27.1 us -> 31.9 us  [from_left(): pl.pallas_call(functools.partial(left_kernel, groups), grid=(groups + 1,)...]
    ppermute x1, starting transfers between devices: 9.14 us -> 12.9 us  [shards(): next_before = lax.ppermute(right, 'col', chain(col_devices, 1))]
    unnamed x16 -> x20, local copies, waits for them, and re-layouts: 5.7 us -> 7.42 us
  transfers between devices with their start and end apart: 14 -> 14, of which waited for: 4 -> 2; matrix products, arithmetic and copies ran while one was open for 12% -> 11% of each run, Pallas kernels for 44% -> 47%
where the time goes in v3:
time: 273 us; the launch traced here: 271 us
  Pallas kernels  150 us (55%)
  starting transfers between devices  46.9 us (17%)
  waiting for transfers between devices  32.4 us (12%)
  local copies, waits for them, and re-layouts  23.4 us (9%)
  other arithmetic  17.1 us (6%)
    pallas_call x1, Pallas kernels, inner(): pl.pallas_call(functools.partial(last_kernel, groups), grid=(groups + 1,)...  46.6 us
    pallas_call x2, Pallas kernels, from_left(): pl.pallas_call(functools.partial(left_kernel, groups), grid=(groups + 1,)...  31.9 us
    pallas_call x2, Pallas kernels, outer_columns(): pl.pallas_call(functools.partial(outer_kernel, side), grid=(count,), in_s...  22.8 us
    pallas_call x1, Pallas kernels, middle_columns(): pl.pallas_call(functools.partial(middle_kernel, columns), grid=(height //...  22.7 us
    ppermute x1, waiting for transfers between devices, column_panel(): got = lax.ppermute(other, 'col', [(c, (c + 4) % 8) for c in range(8)])  21 us
    ppermute x1, starting transfers between devices, shards(): next_before = lax.ppermute(right, 'col', chain(col_devices, 1))  12.9 us
    pallas_call x1, Pallas kernels, col_edges(): pl.pallas_call(functools.partial(col_edge_kernel, scale, relayed, with_ri...  12.8 us
    ppermute x1, waiting for transfers between devices, column_panel(): up = lax.ppermute(own, both, pairs([(0, 0, 1), (0, 2, 3), (1, 1, 2)]))  11.3 us
  transfers between devices with their start and end apart: 14, of which 2 were waited for; matrix products, arithmetic and copies ran while one was open for 11% of the time, Pallas kernels for 47%

profile of v3, /device:TPU:1, one launch (start us, length us, event | category | flops | bytes accessed | tf_op | source)
XLA Modules:
  0.0 271.3 jit_solution(17459221298720204181)
XLA Ops:
  2.8 4.0 %collective-permute-start = (f32[256,256]{1,0:T(8,128)S(1)}, f32[256,256]{1,0:T(8,128)S(1)}, u32[]{:S(2)}, u32[]{:S(2)}) collective-permute-start(f32[256,256]{1,0:T(8,128)S(1)} %slice_multiply_fusion), channel_id=1, source_target_pairs={{0,8},{8,16},{16,24},{1,9},{9,17},{17,25},{2,10},{10,18},{18,26},{... | collective-permute-start | bytes 786440 | tf_op jit(solution)/shard_map/ppermute | solution.py:481
  7.7 2.2 select_multiply_fusion
  9.9 4.1 %slice_bitcast_fusion = (f32[1,2048,256]{2,1,0:T(8,128)S(1)}, f32[1,2048,256]{2,1,0:T(8,128)S(1)}, f32[1,2048,256]{2,1,0:T(8,128)S(1)}, f32[1,2048,256]{2,1,0:T(8,128)S(1)}) fusion(f32[2048,1024]{1,0:T(8,128)} %b_ref.1, f32[2048,1024]{1,0:T(8,128)} %a_ref.1), kind=kLoop, calls=%fused_computation.11 | loop fusion | bytes 16777216 | tf_op jit(solution)/shard_map/stack | solution.py:488
  14.0 2.3 pad_maximum_fusion
  16.3 2.3 pad_maximum_fusion.1
  18.9 4.2 %collective-permute-start.1 = (f32[640,384]{1,0:T(8,128)S(1)}, f32[640,384]{1,0:T(8,128)S(1)}, u32[]{:S(2)}, u32[]{:S(2)}) collective-permute-start(f32[640,384]{1,0:T(8,128)S(1)} %constant_dynamic-slice_fusion), channel_id=1, source_target_pairs={{0,16},{1,17},{4,20},{5,21},{16,0},{17,1},{20,4},{21,5},{10,26},{1... | collective-permute-start | bytes 2949128 | tf_op jit(solution)/shard_map/ppermute | solution.py:460
  25.2 1.9 collective-permute-start.9
  27.1 4.5 %collective-permute-start.6 = (f32[2,2048,256]{2,1,0:T(8,128)}, f32[2,2048,256]{2,1,0:T(8,128)}, u32[]{:S(2)}, u32[]{:S(2)}) collective-permute-start(f32[2,2048,256]{2,1,0:T(8,128)} %pad_maximum_fusion), channel_id=1, source_target_pairs={{1,0},{2,1},{3,2},{4,3},{5,4},{6,5},{7,6},{9,8},{10,9},{11,10},{12... | collective-permute-start | bytes 12582920 | tf_op jit(solution)/shard_map/ppermute | solution.py:417
  31.6 1.9 band_rows.1
  33.6 1.7 copy-done
  35.3 1.6 copy-done.1
  36.9 16.0 %from_left.2.pi_ref = f32[2048,1024]{1,0:T(8,128)} custom-call(f32[2048,1024]{1,0:T(8,128)} %a_ref.1, bf16[8,256,768]{2,1,0:T(8,128)(2,1)} %copy-done, bf16[8,256,768]{2,1,0:T(8,128)(2,1)} %copy-done.1), custom_call_target="tpu_custom_call" | custom-call | tf_op jit(solution)/shard_map/from_left/pallas_call | solution.py:265
  52.9 11.3 %collective-permute-done.2 = f32[640,384]{1,0:T(8,128)S(1)} collective-permute-done((f32[640,384]{1,0:T(8,128)S(1)}, f32[640,384]{1,0:T(8,128)S(1)}, u32[]{:S(2)}, u32[]{:S(2)}) %collective-permute-start.2) | collective-permute-done | bytes 983072 | tf_op jit(solution)/shard_map/ppermute | solution.py:461
  66.8 1.7 slice_bitcast_fusion.9
  68.5 1.7 slice_bitcast_fusion.8
  70.2 2.4 pad_maximum_fusion.2
  73.3 2.5 broadcast_select_fusion.2
  75.8 4.2 %collective-permute-start.7 = (f32[2,256,1024]{2,1,0:T(8,128)}, f32[2,256,1024]{2,1,0:T(8,128)S(1)}, u32[]{:S(2)}, u32[]{:S(2)}) collective-permute-start(f32[2,256,1024]{2,1,0:T(8,128)} %get-tuple-element.36), channel_id=1, source_target_pairs={{0,8},{8,16},{16,24},{1,9},{9,17},{17,25},{2,10},{10,18},{18,26},{... | collective-permute-start | bytes 6291464 | tf_op jit(solution)/shard_map/ppermute | solution.py:401
  85.0 15.9 %from_left.3.qi_ref = f32[2048,1024]{1,0:T(8,128)} custom-call(f32[2048,1024]{1,0:T(8,128)} %b_ref.1, bf16[8,256,768]{2,1,0:T(8,128)(2,1)} %copy-done, bf16[8,256,768]{2,1,0:T(8,128)(2,1)} %copy-done.1), custom_call_target="tpu_custom_call" | custom-call | tf_op jit(solution)/shard_map/from_left/pallas_call | solution.py:265
  101.0 21.0 %collective-permute-done.5 = f32[640,384]{1,0:T(8,128)S(1)} collective-permute-done((f32[640,384]{1,0:T(8,128)}, f32[640,384]{1,0:T(8,128)S(1)}, u32[]{:S(2)}, u32[]{:S(2)}) %collective-permute-start.5) | collective-permute-done | bytes 983072 | tf_op jit(solution)/shard_map/ppermute | solution.py:469
  125.5 11.4 %outer_columns.2 = (f32[2048,1024]{1,0:T(8,128)}, f32[2048,1024]{1,0:T(8,128)}, f32[2,2048,256]{2,1,0:T(8,128)}) custom-call(f32[2048,1024]{1,0:T(8,128)} %a_ref.1, f32[2048,1024]{1,0:T(8,128)} %b_ref.1, bf16[4,768,256]{2,1,0:T(8,128)(2,1)} %copy-done.2, bf16[4,768,256]{2,1,0:T(8,128)(2,1)} %copy-done.3, ...), custom_call_target="tpu_custom_call", output_to_operand_aliasing={{0}: (5, {}), {1}: (6, {})} | custom-call | tf_op jit(solution)/shard_map/outer_columns/pallas_call | solution.py:171
  136.9 5.2 %row_edges.2 = (f32[2048,1024]{1,0:T(8,128)}, f32[2048,1024]{1,0:T(8,128)}, f32[2,2048,256]{2,1,0:T(8,128)}) custom-call(bf16[2,256,256]{2,1,0:T(8,128)(2,1)S(1)} %pad_maximum_fusion.9.h_ref, bf16[2,256,256]{2,1,0:T(8,128)(2,1)S(1)} %pad_maximum_fusion.10.l_ref, ...), custom_call_target="tpu_custom_call", output_to_operand_aliasing={{0}: (4, {}), {1}: (5, {}), {2}: (6, {})} | custom-call | tf_op jit(solution)/shard_map/row_edges/pallas_call | solution.py:322
  142.2 11.4 %outer_columns.3 = (f32[2048,1024]{1,0:T(8,128)}, f32[2048,1024]{1,0:T(8,128)}, f32[2,2048,256]{2,1,0:T(8,128)}) custom-call(f32[2048,1024]{1,0:T(8,128)} %a_ref.1, f32[2048,1024]{1,0:T(8,128)} %b_ref.1, bf16[4,768,256]{2,1,0:T(8,128)(2,1)} %copy-done.2, bf16[4,768,256]{2,1,0:T(8,128)(2,1)} %copy-done.3, ...), custom_call_target="tpu_custom_call", output_to_operand_aliasing={{0}: (5, {}), {1}: (6, {})} | custom-call | tf_op jit(solution)/shard_map/outer_columns/pallas_call | solution.py:171
  153.6 12.9 %collective-permute-start.10 = (f32[2,2048,256]{2,1,0:T(8,128)}, f32[2,2048,256]{2,1,0:T(8,128)}, u32[]{:S(2)}, u32[]{:S(2)}) collective-permute-start(f32[2,2048,256]{2,1,0:T(8,128)} %get-tuple-element.44), channel_id=1, source_target_pairs={{0,1},{1,2},{2,3},{3,4},{4,5},{5,6},{6,7},{8,9},{9,10},{10,11},{11... | collective-permute-start | bytes 12582920 | tf_op jit(solution)/shard_map/ppermute | solution.py:521
  166.5 1.9 collective-permute-start.11
  168.4 22.7 %middle_columns.1 = (f32[2048,1024]{1,0:T(8,128)}, f32[2048,1024]{1,0:T(8,128)}) custom-call(f32[2048,1024]{1,0:T(8,128)} %a_ref.1, f32[2048,1024]{1,0:T(8,128)} %b_ref.1, bf16[4,768,256]{2,1,0:T(8,128)(2,1)} %copy-done.2, bf16[4,768,256]{2,1,0:T(8,128)(2,1)} %copy-done.3, ...), custom_call_target="tpu_custom_call", output_to_operand_aliasing={{0}: (4, {}), {1}: (5, {})} | custom-call | tf_op jit(solution)/shard_map/middle_columns/pallas_call | solution.py:216
  191.1 1.7 slice_bitcast_fusion.5
  192.8 1.7 slice_bitcast_fusion.4
  198.8 5.3 %collective-permute-start.12 = (f32[2,256,1024]{2,1,0:T(8,128)}, f32[2,256,1024]{2,1,0:T(8,128)}, u32[]{:S(2)}, u32[]{:S(2)}) collective-permute-start(f32[2,256,1024]{2,1,0:T(8,128)} %pad_maximum_fusion.4), channel_id=1, source_target_pairs={{0,8},{8,16},{16,24},{1,9},{9,17},{17,25},{2,10},{10,18},{18,26},{... | collective-permute-start | bytes 6291464 | tf_op jit(solution)/shard_map/ppermute | solution.py:401
  206.2 46.6 %inner.1 = (f32[2048,1024]{1,0:T(8,128)}, f32[2048,1024]{1,0:T(8,128)}) custom-call(f32[2048,1024]{1,0:T(8,128)} %get-tuple-element.48.p_ref.pf_ref, f32[2048,1024]{1,0:T(8,128)} %get-tuple-element.49.q_ref.qf_ref, bf16[8,256,768]{2,1,0:T(8,128)(2,1)} %copy-done, bf16[8,256,768]{2,1,0:T(8,128)(2,1)} %copy-done.1, bf16[4,768,256]{2,1,0:T(8,128)(2,1)} %copy-done.2, ...), custom_call_target="tpu_custom_call" | custom-call | tf_op jit(solution)/shard_map/inner/pallas_call | solution.py:283
  252.8 5.6 %row_edges.3 = (f32[2048,1024]{1,0:T(8,128)}, f32[2048,1024]{1,0:T(8,128)}) custom-call(bf16[2,256,256]{2,1,0:T(8,128)(2,1)S(1)} %pad_maximum_fusion.9.h_ref, bf16[2,256,256]{2,1,0:T(8,128)(2,1)S(1)} %pad_maximum_fusion.10.l_ref, f32[2,256,1024]{2,1,0:T(8,128)} %collective-permute-done.12.above_ref, ...), custom_call_target="tpu_custom_call", output_to_operand_aliasing={{0}: (4, {}), {1}: (5, {})} | custom-call | tf_op jit(solution)/shard_map/row_edges/pallas_call | solution.py:322
  258.5 12.8 %col_edges.1 = (f32[2048,1024]{1,0:T(8,128)}, f32[2048,1024]{1,0:T(8,128)}) custom-call(s32[2]{0:T(128)S(1)} %add_convert_fusion.use_ref, bf16[2,256,256]{2,1,0:T(8,128)(2,1)S(1)} %pad_maximum_fusion.7.refs_0_, bf16[2,256,256]{2,1,0:T(8,128)(2,1)S(1)} %pad_maximum_fusion.8.refs_1_, ...), custom_call_target="tpu_custom_call", output_to_operand_aliasing={{0}: (5, {}), {1}: (6, {})} | custom-call | tf_op jit(solution)/shard_map/col_edges/pallas_call | solution.py:380
  (63 shorter events, 23.4 us)
Async XLA Ops:
  2.8 15.8 %collective-permute-start = (f32[256,256]{1,0:T(8,128)S(1)}, f32[256,256]{1,0:T(8,128)S(1)}, u32[]{:S(2)}, u32[]{:S(2)}) collective-permute-start(f32[256,256]{1,0:T(8,128)S(1)} %slice_multiply_fusion), channel_id=1, source_target_pairs={{0,8},{8,16},{16,24},{1,9},{9,17},{17,25},{2,10},{10,18},{18,26},{... | collective-permute-start | bytes 786440 | tf_op jit(solution)/shard_map/ppermute | solution.py:481
  18.9 34.0 %collective-permute-start.1 = (f32[640,384]{1,0:T(8,128)S(1)}, f32[640,384]{1,0:T(8,128)S(1)}, u32[]{:S(2)}, u32[]{:S(2)}) collective-permute-start(f32[640,384]{1,0:T(8,128)S(1)} %constant_dynamic-slice_fusion), channel_id=1, source_target_pairs={{0,16},{1,17},{4,20},{5,21},{16,0},{17,1},{20,4},{21,5},{10,26},{1... | collective-permute-start | bytes 2949128 | tf_op jit(solution)/shard_map/ppermute | solution.py:460
  23.1 41.1 %collective-permute-start.2 = (f32[640,384]{1,0:T(8,128)S(1)}, f32[640,384]{1,0:T(8,128)S(1)}, u32[]{:S(2)}, u32[]{:S(2)}) collective-permute-start(f32[640,384]{1,0:T(8,128)S(1)} %constant_dynamic-slice_fusion), channel_id=1, source_target_pairs={{0,8},{1,9},{4,12},{5,13},{16,24},{17,25},{20,28},{21,29},{10,18},... | collective-permute-start | bytes 2949128 | tf_op jit(solution)/shard_map/ppermute | solution.py:461
  24.5 39.8 %collective-permute-start.3 = (f32[640,384]{1,0:T(8,128)S(1)}, f32[640,384]{1,0:T(8,128)S(1)}, u32[]{:S(2)}, u32[]{:S(2)}) collective-permute-start(f32[640,384]{1,0:T(8,128)S(1)} %constant_dynamic-slice_fusion), channel_id=1, source_target_pairs={{16,8},{17,9},{20,12},{21,13},{10,2},{11,3},{14,6},{15,7},{26,18},... | collective-permute-start | bytes 2949128 | tf_op jit(solution)/shard_map/ppermute | solution.py:462
  25.2 100.3 %collective-permute-start.9 = (f32[2,2048,256]{2,1,0:T(8,128)}, f32[2,2048,256]{2,1,0:T(8,128)}, u32[]{:S(2)}, u32[]{:S(2)}) collective-permute-start(f32[2,2048,256]{2,1,0:T(8,128)} %pad_maximum_fusion.1), channel_id=1, source_target_pairs={{0,1},{1,2},{2,3},{3,4},{4,5},{5,6},{6,7},{8,9},{9,10},{10,11},{11... | collective-permute-start | bytes 12582920 | tf_op jit(solution)/shard_map/ppermute | solution.py:416
  27.1 115.1 %collective-permute-start.6 = (f32[2,2048,256]{2,1,0:T(8,128)}, f32[2,2048,256]{2,1,0:T(8,128)}, u32[]{:S(2)}, u32[]{:S(2)}) collective-permute-start(f32[2,2048,256]{2,1,0:T(8,128)} %pad_maximum_fusion), channel_id=1, source_target_pairs={{1,0},{2,1},{3,2},{4,3},{5,4},{6,5},{7,6},{9,8},{10,9},{11,10},{12... | collective-permute-start | bytes 12582920 | tf_op jit(solution)/shard_map/ppermute | solution.py:417
  33.6 1.7 copy-start
  35.3 1.6 copy-start.1
  52.9 17.3 %copy-start.4 = (f32[640,384]{1,0:T(8,128)}, f32[640,384]{1,0:T(8,128)S(1)}, u32[]{:S(2)}) copy-start(f32[640,384]{1,0:T(8,128)S(1)} %collective-permute-done.1) | copy-start | bytes 2949124
  64.2 6.0 %copy-start.6 = (f32[640,384]{1,0:T(8,128)}, f32[640,384]{1,0:T(8,128)S(1)}, u32[]{:S(2)}) copy-start(f32[640,384]{1,0:T(8,128)S(1)} %collective-permute-done.2) | copy-start | bytes 2949124
  64.2 1.0 copy-start.8
  65.2 7.4 %collective-permute-start.4 = (f32[640,384]{1,0:T(8,128)S(1)}, f32[640,384]{1,0:T(8,128)}, u32[]{:S(2)}, u32[]{:S(2)}) collective-permute-start(f32[640,384]{1,0:T(8,128)S(1)} %collective-permute-done.1), channel_id=1, source_target_pairs={{16,24},{17,25},{20,28},{21,29},{10,2},{11,3},{14,6},{15,7}} | collective-permute-start | bytes 2949128 | tf_op jit(solution)/shard_map/ppermute | solution.py:464
  70.2 2.4 copy-start.5
  70.2 2.4 copy-start.7
  70.2 3.1 %copy-start.9 = (f32[640,384]{1,0:T(8,128)S(1)}, f32[640,384]{1,0:T(8,128)}, u32[]{:S(2)}) copy-start(f32[640,384]{1,0:T(8,128)} %copy-done.8) | copy-start | bytes 2949124
  75.8 61.1 %collective-permute-start.7 = (f32[2,256,1024]{2,1,0:T(8,128)}, f32[2,256,1024]{2,1,0:T(8,128)S(1)}, u32[]{:S(2)}, u32[]{:S(2)}) collective-permute-start(f32[2,256,1024]{2,1,0:T(8,128)} %get-tuple-element.36), channel_id=1, source_target_pairs={{0,8},{8,16},{16,24},{1,9},{9,17},{17,25},{2,10},{10,18},{18,26},{... | collective-permute-start | bytes 6291464 | tf_op jit(solution)/shard_map/ppermute | solution.py:401
  80.1 56.9 %collective-permute-start.8 = (f32[2,256,1024]{2,1,0:T(8,128)}, f32[2,256,1024]{2,1,0:T(8,128)S(1)}, u32[]{:S(2)}, u32[]{:S(2)}) collective-permute-start(f32[2,256,1024]{2,1,0:T(8,128)} %get-tuple-element.37), channel_id=1, source_target_pairs={{8,0},{16,8},{24,16},{9,1},{17,9},{25,17},{10,2},{18,10},{26,18},{... | collective-permute-start | bytes 6291464 | tf_op jit(solution)/shard_map/ppermute | solution.py:402
  81.5 40.4 %collective-permute-start.5 = (f32[640,384]{1,0:T(8,128)}, f32[640,384]{1,0:T(8,128)S(1)}, u32[]{:S(2)}, u32[]{:S(2)}) collective-permute-start(f32[640,384]{1,0:T(8,128)} %get-tuple-element.54), channel_id=1, source_target_pairs={{0,4},{1,5},{2,6},{3,7},{4,0},{5,1},{6,2},{7,3},{8,12},{9,13},{10,... | collective-permute-start | bytes 2949128 | tf_op jit(solution)/shard_map/ppermute | solution.py:469
  123.1 1.2 copy-start.2
  124.3 1.2 copy-start.3
  153.6 104.9 %collective-permute-start.10 = (f32[2,2048,256]{2,1,0:T(8,128)}, f32[2,2048,256]{2,1,0:T(8,128)}, u32[]{:S(2)}, u32[]{:S(2)}) collective-permute-start(f32[2,2048,256]{2,1,0:T(8,128)} %get-tuple-element.44), channel_id=1, source_target_pairs={{0,1},{1,2},{2,3},{3,4},{4,5},{5,6},{6,7},{8,9},{9,10},{10,11},{11... | collective-permute-start | bytes 12582920 | tf_op jit(solution)/shard_map/ppermute | solution.py:521
  166.5 92.0 %collective-permute-start.11 = (f32[2,2048,256]{2,1,0:T(8,128)}, f32[2,2048,256]{2,1,0:T(8,128)}, u32[]{:S(2)}, u32[]{:S(2)}) collective-permute-start(f32[2,2048,256]{2,1,0:T(8,128)} %get-tuple-element.45), channel_id=1, source_target_pairs={{1,0},{2,1},{3,2},{4,3},{5,4},{6,5},{7,6},{9,8},{10,9},{11,10},{12... | collective-permute-start | bytes 12582920 | tf_op jit(solution)/shard_map/ppermute | solution.py:519
  196.0 56.9 %collective-permute-start.13 = (f32[2,256,1024]{2,1,0:T(8,128)}, f32[2,256,1024]{2,1,0:T(8,128)S(1)}, u32[]{:S(2)}, u32[]{:S(2)}) collective-permute-start(f32[2,256,1024]{2,1,0:T(8,128)} %pad_maximum_fusion.5), channel_id=1, source_target_pairs={{8,0},{16,8},{24,16},{9,1},{17,9},{25,17},{10,2},{18,10},{26,18},{... | collective-permute-start | bytes 6291464 | tf_op jit(solution)/shard_map/ppermute | solution.py:402
  198.8 54.1 %collective-permute-start.12 = (f32[2,256,1024]{2,1,0:T(8,128)}, f32[2,256,1024]{2,1,0:T(8,128)}, u32[]{:S(2)}, u32[]{:S(2)}) collective-permute-start(f32[2,256,1024]{2,1,0:T(8,128)} %pad_maximum_fusion.4), channel_id=1, source_target_pairs={{0,8},{8,16},{16,24},{1,9},{9,17},{17,25},{2,10},{10,18},{18,26},{... | collective-permute-start | bytes 6291464 | tf_op jit(solution)/shard_map/ppermute | solution.py:401

commit v4 on v3

--- a/solution.py
+++ b/solution.py
@@ -183,24 +183,15 @@
 
 
 def middle_kernel(columns, p_ref, q_ref, ch_ref, cl_ref, pi_ref, qi_ref, po_ref, qo_ref, rows):
-    n = pl.program_id(1)
-    height = p_ref.shape[0]
-
-    @pl.when(n == 0)
-    def _():
-        for k, x_ref in enumerate((p_ref, q_ref)):
-            rows[k], rows[k + 2] = split(x_ref[...])
-
-    def product(at):
-        window = slice((at - 1) * G, (at + 2) * G)
-        high = rows[:2, :, window].reshape(2 * height, 3 * G)
-        low = rows[2:, :, window].reshape(2 * height, 3 * G)
-        right = three(high, low, ch_ref[at], cl_ref[at])
-        po_ref[...] = pi_ref[...] - right[:height]
-        qo_ref[...] = qi_ref[...] - right[height:]
-
-    for at in range(1, columns - 1):
-        pl.when(n == at - 1)(functools.partial(product, at))
+    for k, x_ref in enumerate((p_ref, q_ref)):
+        rows[k], rows[k + 2] = split(x_ref[...])
+    for n in range(1, columns - 1):
+        at = slice((n - 1) * G, n * G)
+        right = right_product(
+            lambda w: rows[:, :, w].reshape(4 * G, w.stop - w.start), n, columns, ch_ref, cl_ref
+        )
+        po_ref[:, at] = pi_ref[:, at] - right[:G]
+        qo_ref[:, at] = qi_ref[:, at] - right[G:]
 
 
 def middle_columns(p, q, col_band, p_left, q_left):
@@ -208,19 +199,18 @@
     columns = width // G
     if columns <= 2:
         return p_left, q_left
-    rows = min(height, 2 * G)
-    whole = pl.BlockSpec((rows, width), lambda i, n: (i, 0))
-    band = pl.BlockSpec(col_band[0].shape, lambda i, n: (0, 0, 0))
-    tile = pl.BlockSpec((rows, G), lambda i, n: (i, n + 1))
+    whole = pl.BlockSpec((G, width), lambda i: (i, 0))
+    band = pl.BlockSpec(col_band[0].shape, lambda i: (0, 0, 0))
+    tile = pl.BlockSpec((pl.Element(G), pl.Element(width - 2 * G)), lambda i: (i * G, G))
     out = jax.ShapeDtypeStruct(p.shape, F32)
     return pl.pallas_call(
         functools.partial(middle_kernel, columns),
-        grid=(height // rows, columns - 2),
+        grid=(height // G,),
         in_specs=[whole, whole, band, band, tile, tile],
         out_specs=[tile, tile],
         out_shape=[out, out],
         input_output_aliases={4: 0, 5: 1},
-        scratch_shapes=[pltpu.VMEM((4, rows, width), BF16)],
+        scratch_shapes=[pltpu.VMEM((4, G, width), BF16)],
         compiler_params=pltpu.CompilerParams(vmem_limit_bytes=56 << 20),
         cost_estimate=pl.CostEstimate(flops=0, bytes_accessed=0, transcendentals=0),
         name="middle_columns",

time: 273 us -> 270 us (0.989)
  Pallas kernels: 150 us -> 146 us
    pallas_call x1, Pallas kernels: 22.7 us -> 18 us  [middle_columns(): pl.pallas_call(functools.partial(middle_kernel, columns), grid=(height //...]
  transfers between devices with their start and end apart: 14 -> 14, of which waited for: 2 -> 3; matrix products, arithmetic and copies ran while one was open for 11% -> 11% of each run, Pallas kernels for 47% -> 45%
where the time goes in v4:
time: 270 us; the launch traced here: 269 us
  Pallas kernels  146 us (54%)
  starting transfers between devices  46.9 us (17%)
  waiting for transfers between devices  34.5 us (13%)
  local copies, waits for them, and re-layouts  23.4 us (9%)
  other arithmetic  17.1 us (6%)
    pallas_call x1, Pallas kernels, inner(): pl.pallas_call(functools.partial(last_kernel, groups), grid=(groups + 1,)...  46.6 us
    pallas_call x2, Pallas kernels, from_left(): pl.pallas_call(functools.partial(left_kernel, groups), grid=(groups + 1,)...  31.9 us
    pallas_call x2, Pallas kernels, outer_columns(): pl.pallas_call(functools.partial(outer_kernel, side), grid=(count,), in_s...  22.8 us
    ppermute x1, waiting for transfers between devices, column_panel(): got = lax.ppermute(other, 'col', [(c, (c + 4) % 8) for c in range(8)])  21 us
    pallas_call x1, Pallas kernels, middle_columns(): pl.pallas_call(functools.partial(middle_kernel, columns), grid=(height //...  18 us
    ppermute x1, starting transfers between devices, shards(): next_before = lax.ppermute(right, 'col', chain(col_devices, 1))  12.9 us
    pallas_call x1, Pallas kernels, col_edges(): pl.pallas_call(functools.partial(col_edge_kernel, scale, relayed, with_ri...  12.8 us
    ppermute x1, waiting for transfers between devices, column_panel(): up = lax.ppermute(own, both, pairs([(0, 0, 1), (0, 2, 3), (1, 1, 2)]))  11.3 us
  transfers between devices with their start and end apart: 14, of which 3 were waited for; matrix products, arithmetic and copies ran while one was open for 11% of the time, Pallas kernels for 45%

profile of v4, /device:TPU:1, one launch (start us, length us, event | category | flops | bytes accessed | tf_op | source)
XLA Modules:
  0.0 268.8 jit_solution(6938706354283808535)
XLA Ops:
  2.8 4.0 %collective-permute-start = (f32[256,256]{1,0:T(8,128)S(1)}, f32[256,256]{1,0:T(8,128)S(1)}, u32[]{:S(2)}, u32[]{:S(2)}) collective-permute-start(f32[256,256]{1,0:T(8,128)S(1)} %slice_multiply_fusion), channel_id=1, source_target_pairs={{0,8},{8,16},{16,24},{1,9},{9,17},{17,25},{2,10},{10,18},{18,26},{... | collective-permute-start | bytes 786440 | tf_op jit(solution)/shard_map/ppermute | solution.py:471
  7.7 2.2 select_multiply_fusion
  9.9 4.1 %slice_bitcast_fusion = (f32[1,2048,256]{2,1,0:T(8,128)S(1)}, f32[1,2048,256]{2,1,0:T(8,128)S(1)}, f32[1,2048,256]{2,1,0:T(8,128)S(1)}, f32[1,2048,256]{2,1,0:T(8,128)S(1)}) fusion(f32[2048,1024]{1,0:T(8,128)} %b_ref.1, f32[2048,1024]{1,0:T(8,128)} %a_ref.1), kind=kLoop, calls=%fused_computation.11 | loop fusion | bytes 16777216 | tf_op jit(solution)/shard_map/stack | solution.py:478
  14.0 2.3 pad_maximum_fusion
  16.3 2.3 pad_maximum_fusion.1
  18.9 4.2 %collective-permute-start.1 = (f32[640,384]{1,0:T(8,128)S(1)}, f32[640,384]{1,0:T(8,128)S(1)}, u32[]{:S(2)}, u32[]{:S(2)}) collective-permute-start(f32[640,384]{1,0:T(8,128)S(1)} %constant_dynamic-slice_fusion), channel_id=1, source_target_pairs={{0,16},{1,17},{4,20},{5,21},{16,0},{17,1},{20,4},{21,5},{10,26},{1... | collective-permute-start | bytes 2949128 | tf_op jit(solution)/shard_map/ppermute | solution.py:450
  25.2 1.9 collective-permute-start.9
  27.1 4.5 %collective-permute-start.6 = (f32[2,2048,256]{2,1,0:T(8,128)}, f32[2,2048,256]{2,1,0:T(8,128)}, u32[]{:S(2)}, u32[]{:S(2)}) collective-permute-start(f32[2,2048,256]{2,1,0:T(8,128)} %pad_maximum_fusion), channel_id=1, source_target_pairs={{1,0},{2,1},{3,2},{4,3},{5,4},{6,5},{7,6},{9,8},{10,9},{11,10},{12... | collective-permute-start | bytes 12582920 | tf_op jit(solution)/shard_map/ppermute | solution.py:407
  31.6 1.9 band_rows.1
  33.6 1.7 copy-done
  36.9 16.0 %from_left.2.pi_ref = f32[2048,1024]{1,0:T(8,128)} custom-call(f32[2048,1024]{1,0:T(8,128)} %a_ref.1, bf16[8,256,768]{2,1,0:T(8,128)(2,1)} %copy-done, bf16[8,256,768]{2,1,0:T(8,128)(2,1)} %copy-done.1), custom_call_target="tpu_custom_call" | custom-call | tf_op jit(solution)/shard_map/from_left/pallas_call | solution.py:255
  52.9 11.3 %collective-permute-done.2 = f32[640,384]{1,0:T(8,128)S(1)} collective-permute-done((f32[640,384]{1,0:T(8,128)S(1)}, f32[640,384]{1,0:T(8,128)S(1)}, u32[]{:S(2)}, u32[]{:S(2)}) %collective-permute-start.2) | collective-permute-done | bytes 983072 | tf_op jit(solution)/shard_map/ppermute | solution.py:451
  66.8 1.7 slice_bitcast_fusion.9
  68.5 1.7 slice_bitcast_fusion.8
  70.2 2.4 pad_maximum_fusion.2
  73.3 2.5 broadcast_select_fusion.2
  75.8 4.2 %collective-permute-start.7 = (f32[2,256,1024]{2,1,0:T(8,128)}, f32[2,256,1024]{2,1,0:T(8,128)S(1)}, u32[]{:S(2)}, u32[]{:S(2)}) collective-permute-start(f32[2,256,1024]{2,1,0:T(8,128)} %get-tuple-element.36), channel_id=1, source_target_pairs={{0,8},{8,16},{16,24},{1,9},{9,17},{17,25},{2,10},{10,18},{18,26},{... | collective-permute-start | bytes 6291464 | tf_op jit(solution)/shard_map/ppermute | solution.py:391
  85.0 15.9 %from_left.3.qi_ref = f32[2048,1024]{1,0:T(8,128)} custom-call(f32[2048,1024]{1,0:T(8,128)} %b_ref.1, bf16[8,256,768]{2,1,0:T(8,128)(2,1)} %copy-done, bf16[8,256,768]{2,1,0:T(8,128)(2,1)} %copy-done.1), custom_call_target="tpu_custom_call" | custom-call | tf_op jit(solution)/shard_map/from_left/pallas_call | solution.py:255
  101.0 21.0 %collective-permute-done.5 = f32[640,384]{1,0:T(8,128)S(1)} collective-permute-done((f32[640,384]{1,0:T(8,128)}, f32[640,384]{1,0:T(8,128)S(1)}, u32[]{:S(2)}, u32[]{:S(2)}) %collective-permute-start.5) | collective-permute-done | bytes 983072 | tf_op jit(solution)/shard_map/ppermute | solution.py:459
  125.5 11.4 %outer_columns.2 = (f32[2048,1024]{1,0:T(8,128)}, f32[2048,1024]{1,0:T(8,128)}, f32[2,2048,256]{2,1,0:T(8,128)}) custom-call(f32[2048,1024]{1,0:T(8,128)} %a_ref.1, f32[2048,1024]{1,0:T(8,128)} %b_ref.1, bf16[4,768,256]{2,1,0:T(8,128)(2,1)} %copy-done.2, bf16[4,768,256]{2,1,0:T(8,128)(2,1)} %copy-done.3, ...), custom_call_target="tpu_custom_call", output_to_operand_aliasing={{0}: (5, {}), {1}: (6, {})} | custom-call | tf_op jit(solution)/shard_map/outer_columns/pallas_call | solution.py:171
  136.9 5.2 %row_edges.2 = (f32[2048,1024]{1,0:T(8,128)}, f32[2048,1024]{1,0:T(8,128)}, f32[2,2048,256]{2,1,0:T(8,128)}) custom-call(bf16[2,256,256]{2,1,0:T(8,128)(2,1)S(1)} %pad_maximum_fusion.9.h_ref, bf16[2,256,256]{2,1,0:T(8,128)(2,1)S(1)} %pad_maximum_fusion.10.l_ref, ...), custom_call_target="tpu_custom_call", output_to_operand_aliasing={{0}: (4, {}), {1}: (5, {}), {2}: (6, {})} | custom-call | tf_op jit(solution)/shard_map/row_edges/pallas_call | solution.py:312
  142.2 11.4 %outer_columns.3 = (f32[2048,1024]{1,0:T(8,128)}, f32[2048,1024]{1,0:T(8,128)}, f32[2,2048,256]{2,1,0:T(8,128)}) custom-call(f32[2048,1024]{1,0:T(8,128)} %a_ref.1, f32[2048,1024]{1,0:T(8,128)} %b_ref.1, bf16[4,768,256]{2,1,0:T(8,128)(2,1)} %copy-done.2, bf16[4,768,256]{2,1,0:T(8,128)(2,1)} %copy-done.3, ...), custom_call_target="tpu_custom_call", output_to_operand_aliasing={{0}: (5, {}), {1}: (6, {})} | custom-call | tf_op jit(solution)/shard_map/outer_columns/pallas_call | solution.py:171
  153.6 12.9 %collective-permute-start.10 = (f32[2,2048,256]{2,1,0:T(8,128)}, f32[2,2048,256]{2,1,0:T(8,128)}, u32[]{:S(2)}, u32[]{:S(2)}) collective-permute-start(f32[2,2048,256]{2,1,0:T(8,128)} %get-tuple-element.44), channel_id=1, source_target_pairs={{0,1},{1,2},{2,3},{3,4},{4,5},{5,6},{6,7},{8,9},{9,10},{10,11},{11... | collective-permute-start | bytes 12582920 | tf_op jit(solution)/shard_map/ppermute | solution.py:511
  166.5 1.9 collective-permute-start.11
  168.4 18.0 %middle_columns.1 = (f32[2048,1024]{1,0:T(8,128)}, f32[2048,1024]{1,0:T(8,128)}) custom-call(f32[2048,1024]{1,0:T(8,128)} %a_ref.1, f32[2048,1024]{1,0:T(8,128)} %b_ref.1, bf16[4,768,256]{2,1,0:T(8,128)(2,1)} %copy-done.2, bf16[4,768,256]{2,1,0:T(8,128)(2,1)} %copy-done.3, ...), custom_call_target="tpu_custom_call", output_to_operand_aliasing={{0}: (4, {}), {1}: (5, {})} | custom-call | tf_op jit(solution)/shard_map/middle_columns/pallas_call | solution.py:206
  186.4 1.7 slice_bitcast_fusion.5
  188.1 1.7 slice_bitcast_fusion.4
  194.1 5.3 %collective-permute-start.12 = (f32[2,256,1024]{2,1,0:T(8,128)}, f32[2,256,1024]{2,1,0:T(8,128)}, u32[]{:S(2)}, u32[]{:S(2)}) collective-permute-start(f32[2,256,1024]{2,1,0:T(8,128)} %pad_maximum_fusion.4), channel_id=1, source_target_pairs={{0,8},{8,16},{16,24},{1,9},{9,17},{17,25},{2,10},{10,18},{18,26},{... | collective-permute-start | bytes 6291464 | tf_op jit(solution)/shard_map/ppermute | solution.py:391
  201.6 46.6 %inner.1 = (f32[2048,1024]{1,0:T(8,128)}, f32[2048,1024]{1,0:T(8,128)}) custom-call(f32[2048,1024]{1,0:T(8,128)} %get-tuple-element.48.p_ref.pf_ref, f32[2048,1024]{1,0:T(8,128)} %get-tuple-element.49.q_ref.qf_ref, bf16[8,256,768]{2,1,0:T(8,128)(2,1)} %copy-done, bf16[8,256,768]{2,1,0:T(8,128)(2,1)} %copy-done.1, bf16[4,768,256]{2,1,0:T(8,128)(2,1)} %copy-done.2, ...), custom_call_target="tpu_custom_call" | custom-call | tf_op jit(solution)/shard_map/inner/pallas_call | solution.py:273
  248.2 5.6 %row_edges.3 = (f32[2048,1024]{1,0:T(8,128)}, f32[2048,1024]{1,0:T(8,128)}) custom-call(bf16[2,256,256]{2,1,0:T(8,128)(2,1)S(1)} %pad_maximum_fusion.9.h_ref, bf16[2,256,256]{2,1,0:T(8,128)(2,1)S(1)} %pad_maximum_fusion.10.l_ref, f32[2,256,1024]{2,1,0:T(8,128)} %collective-permute-done.12.above_ref, ...), custom_call_target="tpu_custom_call", output_to_operand_aliasing={{0}: (4, {}), {1}: (5, {})} | custom-call | tf_op jit(solution)/shard_map/row_edges/pallas_call | solution.py:312
  253.8 2.1 collective-permute-done.11.refs_3_
  255.9 12.8 %col_edges.1 = (f32[2048,1024]{1,0:T(8,128)}, f32[2048,1024]{1,0:T(8,128)}) custom-call(s32[2]{0:T(128)S(1)} %add_convert_fusion.use_ref, bf16[2,256,256]{2,1,0:T(8,128)(2,1)S(1)} %pad_maximum_fusion.7.refs_0_, bf16[2,256,256]{2,1,0:T(8,128)(2,1)S(1)} %pad_maximum_fusion.8.refs_1_, ...), custom_call_target="tpu_custom_call", output_to_operand_aliasing={{0}: (5, {}), {1}: (6, {})} | custom-call | tf_op jit(solution)/shard_map/col_edges/pallas_call | solution.py:370
  (63 shorter events, 25.1 us)
Async XLA Ops:
  2.8 15.8 %collective-permute-start = (f32[256,256]{1,0:T(8,128)S(1)}, f32[256,256]{1,0:T(8,128)S(1)}, u32[]{:S(2)}, u32[]{:S(2)}) collective-permute-start(f32[256,256]{1,0:T(8,128)S(1)} %slice_multiply_fusion), channel_id=1, source_target_pairs={{0,8},{8,16},{16,24},{1,9},{9,17},{17,25},{2,10},{10,18},{18,26},{... | collective-permute-start | bytes 786440 | tf_op jit(solution)/shard_map/ppermute | solution.py:471
  18.9 34.0 %collective-permute-start.1 = (f32[640,384]{1,0:T(8,128)S(1)}, f32[640,384]{1,0:T(8,128)S(1)}, u32[]{:S(2)}, u32[]{:S(2)}) collective-permute-start(f32[640,384]{1,0:T(8,128)S(1)} %constant_dynamic-slice_fusion), channel_id=1, source_target_pairs={{0,16},{1,17},{4,20},{5,21},{16,0},{17,1},{20,4},{21,5},{10,26},{1... | collective-permute-start | bytes 2949128 | tf_op jit(solution)/shard_map/ppermute | solution.py:450
  23.1 41.1 %collective-permute-start.2 = (f32[640,384]{1,0:T(8,128)S(1)}, f32[640,384]{1,0:T(8,128)S(1)}, u32[]{:S(2)}, u32[]{:S(2)}) collective-permute-start(f32[640,384]{1,0:T(8,128)S(1)} %constant_dynamic-slice_fusion), channel_id=1, source_target_pairs={{0,8},{1,9},{4,12},{5,13},{16,24},{17,25},{20,28},{21,29},{10,18},... | collective-permute-start | bytes 2949128 | tf_op jit(solution)/shard_map/ppermute | solution.py:451
  24.5 39.8 %collective-permute-start.3 = (f32[640,384]{1,0:T(8,128)S(1)}, f32[640,384]{1,0:T(8,128)S(1)}, u32[]{:S(2)}, u32[]{:S(2)}) collective-permute-start(f32[640,384]{1,0:T(8,128)S(1)} %constant_dynamic-slice_fusion), channel_id=1, source_target_pairs={{16,8},{17,9},{20,12},{21,13},{10,2},{11,3},{14,6},{15,7},{26,18},... | collective-permute-start | bytes 2949128 | tf_op jit(solution)/shard_map/ppermute | solution.py:452
  25.2 100.3 %collective-permute-start.9 = (f32[2,2048,256]{2,1,0:T(8,128)}, f32[2,2048,256]{2,1,0:T(8,128)}, u32[]{:S(2)}, u32[]{:S(2)}) collective-permute-start(f32[2,2048,256]{2,1,0:T(8,128)} %pad_maximum_fusion.1), channel_id=1, source_target_pairs={{0,1},{1,2},{2,3},{3,4},{4,5},{5,6},{6,7},{8,9},{9,10},{10,11},{11... | collective-permute-start | bytes 12582920 | tf_op jit(solution)/shard_map/ppermute | solution.py:406
  27.1 115.1 %collective-permute-start.6 = (f32[2,2048,256]{2,1,0:T(8,128)}, f32[2,2048,256]{2,1,0:T(8,128)}, u32[]{:S(2)}, u32[]{:S(2)}) collective-permute-start(f32[2,2048,256]{2,1,0:T(8,128)} %pad_maximum_fusion), channel_id=1, source_target_pairs={{1,0},{2,1},{3,2},{4,3},{5,4},{6,5},{7,6},{9,8},{10,9},{11,10},{12... | collective-permute-start | bytes 12582920 | tf_op jit(solution)/shard_map/ppermute | solution.py:407
  33.6 1.7 copy-start
  35.3 1.6 copy-start.1
  52.9 17.3 %copy-start.4 = (f32[640,384]{1,0:T(8,128)}, f32[640,384]{1,0:T(8,128)S(1)}, u32[]{:S(2)}) copy-start(f32[640,384]{1,0:T(8,128)S(1)} %collective-permute-done.1) | copy-start | bytes 2949124
  64.2 6.0 %copy-start.6 = (f32[640,384]{1,0:T(8,128)}, f32[640,384]{1,0:T(8,128)S(1)}, u32[]{:S(2)}) copy-start(f32[640,384]{1,0:T(8,128)S(1)} %collective-permute-done.2) | copy-start | bytes 2949124
  64.2 1.0 copy-start.8
  65.2 7.4 %collective-permute-start.4 = (f32[640,384]{1,0:T(8,128)S(1)}, f32[640,384]{1,0:T(8,128)}, u32[]{:S(2)}, u32[]{:S(2)}) collective-permute-start(f32[640,384]{1,0:T(8,128)S(1)} %collective-permute-done.1), channel_id=1, source_target_pairs={{16,24},{17,25},{20,28},{21,29},{10,2},{11,3},{14,6},{15,7}} | collective-permute-start | bytes 2949128 | tf_op jit(solution)/shard_map/ppermute | solution.py:454
  70.2 2.4 copy-start.5
  70.2 2.4 copy-start.7
  70.2 3.1 %copy-start.9 = (f32[640,384]{1,0:T(8,128)S(1)}, f32[640,384]{1,0:T(8,128)}, u32[]{:S(2)}) copy-start(f32[640,384]{1,0:T(8,128)} %copy-done.8) | copy-start | bytes 2949124
  75.8 61.1 %collective-permute-start.7 = (f32[2,256,1024]{2,1,0:T(8,128)}, f32[2,256,1024]{2,1,0:T(8,128)S(1)}, u32[]{:S(2)}, u32[]{:S(2)}) collective-permute-start(f32[2,256,1024]{2,1,0:T(8,128)} %get-tuple-element.36), channel_id=1, source_target_pairs={{0,8},{8,16},{16,24},{1,9},{9,17},{17,25},{2,10},{10,18},{18,26},{... | collective-permute-start | bytes 6291464 | tf_op jit(solution)/shard_map/ppermute | solution.py:391
  80.1 56.9 %collective-permute-start.8 = (f32[2,256,1024]{2,1,0:T(8,128)}, f32[2,256,1024]{2,1,0:T(8,128)S(1)}, u32[]{:S(2)}, u32[]{:S(2)}) collective-permute-start(f32[2,256,1024]{2,1,0:T(8,128)} %get-tuple-element.37), channel_id=1, source_target_pairs={{8,0},{16,8},{24,16},{9,1},{17,9},{25,17},{10,2},{18,10},{26,18},{... | collective-permute-start | bytes 6291464 | tf_op jit(solution)/shard_map/ppermute | solution.py:392
  81.5 40.4 %collective-permute-start.5 = (f32[640,384]{1,0:T(8,128)}, f32[640,384]{1,0:T(8,128)S(1)}, u32[]{:S(2)}, u32[]{:S(2)}) collective-permute-start(f32[640,384]{1,0:T(8,128)} %get-tuple-element.54), channel_id=1, source_target_pairs={{0,4},{1,5},{2,6},{3,7},{4,0},{5,1},{6,2},{7,3},{8,12},{9,13},{10,... | collective-permute-start | bytes 2949128 | tf_op jit(solution)/shard_map/ppermute | solution.py:459
  123.1 1.2 copy-start.2
  124.3 1.2 copy-start.3
  153.6 100.2 %collective-permute-start.10 = (f32[2,2048,256]{2,1,0:T(8,128)}, f32[2,2048,256]{2,1,0:T(8,128)}, u32[]{:S(2)}, u32[]{:S(2)}) collective-permute-start(f32[2,2048,256]{2,1,0:T(8,128)} %get-tuple-element.44), channel_id=1, source_target_pairs={{0,1},{1,2},{2,3},{3,4},{4,5},{5,6},{6,7},{8,9},{9,10},{10,11},{11... | collective-permute-start | bytes 12582920 | tf_op jit(solution)/shard_map/ppermute | solution.py:511
  166.5 89.4 %collective-permute-start.11 = (f32[2,2048,256]{2,1,0:T(8,128)}, f32[2,2048,256]{2,1,0:T(8,128)}, u32[]{:S(2)}, u32[]{:S(2)}) collective-permute-start(f32[2,2048,256]{2,1,0:T(8,128)} %get-tuple-element.45), channel_id=1, source_target_pairs={{1,0},{2,1},{3,2},{4,3},{5,4},{6,5},{7,6},{9,8},{10,9},{11,10},{12... | collective-permute-start | bytes 12582920 | tf_op jit(solution)/shard_map/ppermute | solution.py:509
  191.3 56.9 %collective-permute-start.13 = (f32[2,256,1024]{2,1,0:T(8,128)}, f32[2,256,1024]{2,1,0:T(8,128)S(1)}, u32[]{:S(2)}, u32[]{:S(2)}) collective-permute-start(f32[2,256,1024]{2,1,0:T(8,128)} %pad_maximum_fusion.5), channel_id=1, source_target_pairs={{8,0},{16,8},{24,16},{9,1},{17,9},{25,17},{10,2},{18,10},{26,18},{... | collective-permute-start | bytes 6291464 | tf_op jit(solution)/shard_map/ppermute | solution.py:392
  194.1 54.1 %collective-permute-start.12 = (f32[2,256,1024]{2,1,0:T(8,128)}, f32[2,256,1024]{2,1,0:T(8,128)}, u32[]{:S(2)}, u32[]{:S(2)}) collective-permute-start(f32[2,256,1024]{2,1,0:T(8,128)} %pad_maximum_fusion.4), channel_id=1, source_target_pairs={{0,8},{8,16},{16,24},{1,9},{9,17},{17,25},{2,10},{10,18},{18,26},{... | collective-permute-start | bytes 6291464 | tf_op jit(solution)/shard_map/ppermute | solution.py:391
